TPU v7x, 128 devices: a whole 4x4x4 slice. The times are simulated.
128 devices in a mesh: pipe: 4 (over z_lo, core), ctx: 8 (over x, z_hi), dp: 4 (over y).
Axes of the slice: x: 4, y: 4, z: 4 (z_hi: 2, z_lo: 2; z = z_hi * 2 + z_lo), core: 2. Of those that a mesh axis runs over, the one named last changes fastest.
Arguments:
- down_input: bfloat16 [4, 2048, 1024], P('dp', 'ctx'), may hold values from -6 to 6
- up_input: bfloat16 [4, 2048, 1024], P('dp', 'ctx'), may hold values from -6 to 6
- down_qkv: bfloat16 [4, 1024, 3072], P('pipe'), may hold values from -0.1875 to 0.1875
- up_qkv: bfloat16 [4, 1024, 3072], P('pipe'), may hold values from -0.1875 to 0.1875
- down_gates: bfloat16 [4, 1024, 16], P('pipe'), may hold values from -0.1875 to 0.1875
- up_gates: bfloat16 [4, 1024, 16], P('pipe'), may hold values from -0.1875 to 0.1875
- down_rates: float32 [4, 8], P('pipe'), may hold values from 0.0002 to 0.05
- up_rates: float32 [4, 8], P('pipe'), may hold values from 0.0002 to 0.05
- down_out: bfloat16 [4, 1024, 1024], P('pipe'), may hold values from -0.1875 to 0.1875
- up_out: bfloat16 [4, 1024, 1024], P('pipe'), may hold values from -0.1875 to 0.1875
- down_cotangent: bfloat16 [4, 4, 2048, 1024], P('pipe', 'dp', 'ctx'), may hold values from -0.046875 to 0.046875
- up_cotangent: bfloat16 [4, 4, 2048, 1024], P('pipe', 'dp', 'ctx'), may hold values from -0.046875 to 0.046875
Outputs:
- down_acts: bfloat16 [4, 4, 2048, 1024], P('pipe', 'dp', 'ctx')
- up_acts: bfloat16 [4, 4, 2048, 1024], P('pipe', 'dp', 'ctx')
- out_grad: float32 [4, 1024, 1024], P('pipe', ('ctx', 'dp'))
All inputs are finite; a program needn't handle non-finite values.
Results may differ from a plain program's by a relative error of at most 0.04.
Values may be sent and summed in bfloat16 or wider, within the bound.
A program may use at most 192 MiB of HBM per device.

v0:
```python
import jax
import jax.numpy as jnp
from jax import lax
from jax.sharding import PartitionSpec as P

BLOCK = 64


EPSILON = 1e-06
EXACT = lax.Precision.HIGHEST


def shifted(value, axis, by):
    peers = lax.axis_size(axis)
    pairs = [(i, i + by) for i in range(peers) if 0 <= i + by < peers]
    return lax.ppermute(value, axis, pairs)


def swapped(block, axis, stride):
    count = lax.axis_size(axis)
    route = []
    for low in range(count):
        high = low | 1 << stride
        if high != low and high < count:
            route += [(low, high), (high, low)]
    return lax.ppermute(block, axis, route)


def mean_norm(values):
    return values * lax.rsqrt(jnp.mean(values * values, axis=-1, keepdims=True) + EPSILON)


def unit_norm(values):
    return values * lax.rsqrt(jnp.sum(values * values, axis=-1, keepdims=True) + EPSILON)


def unit_inverse(strict, repeats):
    negated = -strict
    result = jnp.eye(strict.shape[-1], dtype=jnp.float32) + negated
    raised = negated
    for _ in range(repeats):
        raised = jnp.einsum("...ij,...jk->...ik", raised, raised, precision=EXACT)
        result = result + jnp.einsum("...ij,...jk->...ik", result, raised, precision=EXACT)
    return result


def prepare(stream, qkv_weight, gate_weight, decay_rate):
    length = stream.shape[0]
    head_count = decay_rate.shape[0]
    head_dim = qkv_weight.shape[1] // (3 * head_count)
    blocks = length // BLOCK
    normed = mean_norm(stream.astype(jnp.float32)).astype(jnp.bfloat16)
    project = jnp.dot(normed, qkv_weight, preferred_element_type=jnp.float32)
    gating = jnp.dot(normed, gate_weight, preferred_element_type=jnp.float32)
    project = project.reshape(blocks, BLOCK, 3, head_count, head_dim).transpose(2, 0, 3, 1, 4)
    queries = unit_norm(project[0]) * head_dim ** (-0.5)
    key_rows = unit_norm(project[1])
    value_rows = project[2]
    gating = gating.reshape(blocks, BLOCK, 2, head_count).transpose(2, 0, 3, 1)
    strength = jax.nn.sigmoid(gating[0])
    log_decay = -decay_rate[None, :, None] * jax.nn.softplus(gating[1])
    cumulative = jnp.cumsum(log_decay, axis=-1)
    decay_gap = cumulative[..., :, None] - cumulative[..., None, :]
    row_index = lax.broadcasted_iota(jnp.int32, (BLOCK, BLOCK), 0)
    col_index = lax.broadcasted_iota(jnp.int32, (BLOCK, BLOCK), 1)
    strict_lower = row_index > col_index
    lower_diag = row_index >= col_index
    fading = jnp.exp(jnp.where(lower_diag, decay_gap, 0.0))
    key_gram = jnp.einsum("bhid,bhjd->bhij", key_rows, key_rows, precision=EXACT)
    strict = jnp.where(strict_lower, strength[..., :, None] * key_gram * fading, 0.0)
    inverse = unit_inverse(strict, BLOCK.bit_length() - 2) * strength[..., None, :]
    growth = jnp.exp(cumulative)[..., None]
    erase_rows = jnp.einsum("bhij,bhjd->bhid", inverse, key_rows * growth, precision=EXACT)
    target_rows = jnp.einsum("bhij,bhjd->bhid", inverse, value_rows, precision=EXACT)
    query_decay = queries * growth
    scores = jnp.where(
        lower_diag, jnp.einsum("bhid,bhjd->bhij", queries, key_rows, precision=EXACT) * fading, 0.0
    )
    last_decay = cumulative[..., -1:]
    key_tail = key_rows * jnp.exp(last_decay - cumulative)[..., None]
    block_fade = jnp.exp(last_decay)[..., None]
    return (erase_rows, target_rows, query_decay, scores, key_tail, block_fade)


def block_step(memory, pieces):
    erase_rows, target_rows, query_decay, scores, key_tail, block_fade = pieces
    new_values = target_rows - jnp.einsum("hcd,hde->hce", erase_rows, memory, precision=EXACT)
    output = jnp.einsum("hcd,hde->hce", query_decay, memory, precision=EXACT)
    output = output + jnp.einsum("hij,hje->hie", scores, new_values, precision=EXACT)
    memory = block_fade * memory + jnp.einsum("hcd,hce->hde", key_tail, new_values, precision=EXACT)
    return (memory, output)


def finish(stream, outputs, out_weight):
    blocks, head_count, block_len, head_dim = outputs.shape
    normed = (
        mean_norm(outputs).transpose(0, 2, 1, 3).reshape(blocks * block_len, head_count * head_dim)
    )
    normed = normed.astype(jnp.bfloat16)
    updated = stream.astype(jnp.float32) + jnp.dot(
        normed, out_weight, preferred_element_type=jnp.float32
    )
    return (updated.astype(jnp.bfloat16), normed)


def compose_maps(later_map, earlier_map):
    return jnp.einsum("hde,hef->hdf", later_map, earlier_map, precision=EXACT)


def local_section(stream, qkv_weight, gate_weight, decay_rate, out_weight):
    pieces = prepare(stream, qkv_weight, gate_weight, decay_rate)
    head_count = decay_rate.shape[0]
    head_dim = pieces[0].shape[-1]
    identity = jnp.broadcast_to(
        jnp.eye(head_dim, dtype=jnp.float32), (head_count, head_dim, head_dim)
    )
    zeros_state = jnp.zeros((head_count, head_dim, head_dim), jnp.float32)

    def span_map(carry, piece):
        transfer, offset = carry
        erase_rows, target_rows, query_decay, scores, key_tail, block_fade = piece
        step_map = block_fade * identity - jnp.einsum(
            "hcd,hce->hde", key_tail, erase_rows, precision=EXACT
        )
        transfer = compose_maps(step_map, transfer)
        offset = compose_maps(step_map, offset) + jnp.einsum(
            "hcd,hce->hde", key_tail, target_rows, precision=EXACT
        )
        return ((transfer, offset), None)

    (transfer, offset), _ = lax.scan(span_map, (identity, zeros_state), pieces)

    def relay(relay_turn, incoming):
        outgoing = compose_maps(transfer, incoming) + offset
        return shifted(outgoing.astype(jnp.bfloat16), "ctx", 1).astype(outgoing.dtype)

    incoming = lax.fori_loop(0, lax.axis_size("ctx") - 1, relay, zeros_state)
    memory, outputs = lax.scan(block_step, incoming, pieces)
    return finish(stream, outputs, out_weight)


def token_sum(hidden, cotangent):
    return lax.dot_general(
        hidden, cotangent, (((0,), (0,)), ((), ())), preferred_element_type=jnp.float32
    )


def per_device(
    down_input,
    up_input,
    down_qkv,
    up_qkv,
    down_gates,
    up_gates,
    down_rates,
    up_rates,
    down_out,
    up_out,
    down_cotangent,
    up_cotangent,
):
    sections = lax.axis_size("pipe")
    position = lax.axis_index("pipe")
    current_down = down_input[0]
    current_up = up_input[0]
    tokens_here, model_width = current_down.shape
    inner_width = down_out.shape[1]
    result_down = jnp.zeros_like(current_down)
    result_up = jnp.zeros_like(current_down)
    hidden_down = jnp.zeros((tokens_here, inner_width), jnp.bfloat16)
    hidden_up = jnp.zeros((tokens_here, inner_width), jnp.bfloat16)
    down_set = (down_qkv[0], down_gates[0], down_rates[0], down_out[0])
    up_set = (up_qkv[0], up_gates[0], up_rates[0], up_out[0])
    for turn_index in range(sections):
        going_down = position == turn_index
        going_up = position == sections - 1 - turn_index
        stream = jnp.where(going_down, current_down, current_up)
        qkv_weight, gate_weight, decay_rate, out_weight = lax.cond(
            going_down, lambda: down_set, lambda: up_set
        )
        updated, normed = local_section(stream, qkv_weight, gate_weight, decay_rate, out_weight)
        result_down = jnp.where(going_down, updated, result_down)
        result_up = jnp.where(going_up, updated, result_up)
        hidden_down = jnp.where(going_down, normed, hidden_down)
        hidden_up = jnp.where(going_up, normed, hidden_up)
        if turn_index + 1 < sections:
            current_down = shifted(updated, "pipe", 1)
            current_up = shifted(updated, "pipe", -1)
    own_down = token_sum(hidden_down, down_cotangent[0, 0])
    own_up = token_sum(hidden_up, up_cotangent[0, 0])
    pipe_bits = sections.bit_length() - 1
    mirrored = own_up
    for bit_number in range(pipe_bits):
        mirrored = swapped(mirrored.astype(jnp.bfloat16), "pipe", bit_number).astype(mirrored.dtype)
    gradient = lax.psum_scatter(
        (own_down + mirrored).astype(jnp.bfloat16), ("ctx", "dp"), scatter_dimension=0, tiled=True
    ).astype(jnp.float32)
    return (result_down[None, None], result_up[None, None], gradient[None])


def solution(mesh):
    return jax.shard_map(
        per_device,
        mesh=mesh,
        in_specs=(
            P("dp", "ctx", None),
            P("dp", "ctx", None),
            P("pipe", None, None),
            P("pipe", None, None),
            P("pipe", None, None),
            P("pipe", None, None),
            P("pipe", None),
            P("pipe", None),
            P("pipe", None, None),
            P("pipe", None, None),
            P("pipe", "dp", "ctx", None),
            P("pipe", "dp", "ctx", None),
        ),
        out_specs=(
            P("pipe", "dp", "ctx", None),
            P("pipe", "dp", "ctx", None),
            P("pipe", ("ctx", "dp"), None),
        ),
        check_vma=False,
    )
```

profile of v0, /device:TPU:0, one launch (start us, length us, event | category | flops | bytes accessed | tf_op | source)
XLA Modules:
  0.0 1013.5 jit_solution(9327988667675692577)
XLA Ops:
  7.3 6.0 copy.258
  15.1 7.4 conditional.4
  15.1 6.0 copy.130
  22.5 8.6 copy.57
  66.4 22.2 %while.148 = (s32[]{:T(128)}, f32[8,128,128]{2,1,0:T(8,128)S(1)}, f32[8,128,128]{2,1,0:T(8,128)S(1)}, f32[4,8,1,1]{1,3,2,0:T(1,128)S(1)}, f32[4,8,64,128]{3,2,1,...) while((s32[]{:T(128)}, f32[8,128,128]{2,1,0:T(8,128)S(1)}, ...), condition=%wide.region_6.7_spmd.clone, body=%wide.region_5.6_spmd.clone.sunk | while | flops 604504064 | bytes 7932115 | solution.py:131
  88.6 80.1 %while.149 = (s32[]{:T(128)}, f32[8,128,128]{2,1,0:T(8,128)S(1)}, f32[8,128,128]{2,1,0:T(8,128)S(1)}, f32[8,128,128]{2,1,0:T(8,128)S(1)}, s32[]{:T(128)}, /*index=5*/s32[]{:T(128)}) while((s32[]{:T(128)}, f32[8,128,128]{2,1,0:T(8,128)S(1)}, f32[8,128,128]{2,1,0:T(8,128)S(1)}, f32[8,128,128]{2,1,0:T(8,128)S(1)}, s32[]{:T(128)}, ...), condition=%wide.region_8.9_spmd.clone, body=%wide.region_7.8_spmd.clone.sunk | while | flops 201850880 | bytes 3670135 | solution.py:137
  95.2 6.6 collective-permute-done
  114.8 5.9 collective-permute-start
  126.3 5.9 collective-permute-start
  147.3 6.1 collective-permute-start
  158.0 6.8 collective-permute-start
  168.8 26.7 %while.144 = (s32[]{:T(128)}, f32[8,128,128]{2,1,0:T(8,128)S(1)}, f32[4,8,64,128]{3,2,1,0:T(8,128)S(1)}, f32[4,8,1,1]{1,3,2,0:T(1,128)S(1)}, f32[4,8,64,128]{3,2...) while((s32[]{:T(128)}, f32[8,128,128]{2,1,0:T(8,128)S(1)}, ...), condition=%wide.region_11.12_spmd, body=%wide.region_10.11_spmd.sunk | while | flops 352714752 | bytes 4984009 | solution.py:138
  240.9 22.6 %while.150 = (s32[]{:T(128)}, f32[8,128,128]{2,1,0:T(8,128)S(1)}, f32[8,128,128]{2,1,0:T(8,128)S(1)}, f32[4,8,1,1]{1,3,2,0:T(1,128)S(1)}, f32[4,8,64,128]{3,2,1,...) while((s32[]{:T(128)}, f32[8,128,128]{2,1,0:T(8,128)S(1)}, ...), condition=%wide.region_19.20_spmd.clone, body=%wide.region_18.19_spmd.clone.sunk | while | flops 604504064 | bytes 7932115 | solution.py:131
  263.5 86.6 %while.151 = (s32[]{:T(128)}, f32[8,128,128]{2,1,0:T(8,128)S(1)}, f32[8,128,128]{2,1,0:T(8,128)S(1)}, f32[8,128,128]{2,1,0:T(8,128)S(1)}, s32[]{:T(128)}, /*index=5*/s32[]{:T(128)}) while((s32[]{:T(128)}, f32[8,128,128]{2,1,0:T(8,128)S(1)}, f32[8,128,128]{2,1,0:T(8,128)S(1)}, f32[8,128,128]{2,1,0:T(8,128)S(1)}, s32[]{:T(128)}, ...), condition=%wide.region_21.22_spmd.clone, body=%wide.region_20.21_spmd.clone.sunk | while | flops 201850880 | bytes 3670135 | solution.py:137
  264.1 6.8 collective-permute-start.1
  275.5 6.8 collective-permute-start.1
  286.9 6.8 collective-permute-start.1
  298.3 6.8 collective-permute-start.1
  310.3 7.1 collective-permute-start.1
  323.8 7.1 collective-permute-start.1
  331.0 6.4 collective-permute-done.1
  338.1 6.5 collective-permute-start.1
  350.2 26.5 %while.145 = (s32[]{:T(128)}, f32[8,128,128]{2,1,0:T(8,128)S(1)}, f32[4,8,64,128]{3,2,1,0:T(8,128)S(1)}, f32[4,8,1,1]{1,3,2,0:T(1,128)S(1)}, f32[4,8,64,128]{3,2...) while((s32[]{:T(128)}, f32[8,128,128]{2,1,0:T(8,128)S(1)}, ...), condition=%wide.region_24.25_spmd, body=%wide.region_23.24_spmd.sunk | while | flops 352714752 | bytes 4984009 | solution.py:138
  425.2 22.6 %while.152 = (s32[]{:T(128)}, f32[8,128,128]{2,1,0:T(8,128)S(1)}, f32[8,128,128]{2,1,0:T(8,128)S(1)}, f32[4,8,1,1]{1,3,2,0:T(1,128)S(1)}, f32[4,8,64,128]{3,2,1,...) while((s32[]{:T(128)}, f32[8,128,128]{2,1,0:T(8,128)S(1)}, ...), condition=%wide.region_32.33_spmd.clone, body=%wide.region_31.32_spmd.clone.sunk | while | flops 604504064 | bytes 7932115 | solution.py:131
  447.8 85.5 %while.153 = (s32[]{:T(128)}, f32[8,128,128]{2,1,0:T(8,128)S(1)}, f32[8,128,128]{2,1,0:T(8,128)S(1)}, f32[8,128,128]{2,1,0:T(8,128)S(1)}, s32[]{:T(128)}, /*index=5*/s32[]{:T(128)}) while((s32[]{:T(128)}, f32[8,128,128]{2,1,0:T(8,128)S(1)}, f32[8,128,128]{2,1,0:T(8,128)S(1)}, f32[8,128,128]{2,1,0:T(8,128)S(1)}, s32[]{:T(128)}, ...), condition=%wide.region_34.35_spmd.clone, body=%wide.region_33.34_spmd.clone.sunk | while | flops 201850880 | bytes 3670135 | solution.py:137
  448.4 7.4 collective-permute-start.2
  460.4 6.2 collective-permute-start.2
  471.2 6.8 collective-permute-start.2
  482.6 6.8 collective-permute-start.2
  493.9 6.8 collective-permute-start.2
  506.1 7.1 collective-permute-start.2
  519.7 7.1 collective-permute-start.2
  526.9 6.3 collective-permute-done.2
  533.4 26.5 %while.146 = (s32[]{:T(128)}, f32[8,128,128]{2,1,0:T(8,128)S(1)}, f32[4,8,64,128]{3,2,1,0:T(8,128)S(1)}, f32[4,8,1,1]{1,3,2,0:T(1,128)S(1)}, f32[4,8,64,128]{3,2...) while((s32[]{:T(128)}, f32[8,128,128]{2,1,0:T(8,128)S(1)}, ...), condition=%wide.region_37.38_spmd, body=%wide.region_36.37_spmd.sunk | while | flops 352714752 | bytes 4984009 | solution.py:138
  566.9 9.1 collective-permute-done.9
  612.9 22.4 %while.154 = (s32[]{:T(128)}, f32[8,128,128]{2,1,0:T(8,128)S(1)}, f32[8,128,128]{2,1,0:T(8,128)S(1)}, f32[4,8,1,1]{1,3,2,0:T(1,128)S(1)}, f32[4,8,64,128]{3,2,1,...) while((s32[]{:T(128)}, f32[8,128,128]{2,1,0:T(8,128)S(1)}, ...), condition=%wide.region_45.46_spmd.clone, body=%wide.region_44.45_spmd.clone.sunk | while | flops 604504064 | bytes 7932115 | solution.py:131
  635.4 85.5 %while.155 = (s32[]{:T(128)}, f32[8,128,128]{2,1,0:T(8,128)S(1)}, f32[8,128,128]{2,1,0:T(8,128)S(1)}, f32[8,128,128]{2,1,0:T(8,128)S(1)}, s32[]{:T(128)}, /*index=5*/s32[]{:T(128)}) while((s32[]{:T(128)}, f32[8,128,128]{2,1,0:T(8,128)S(1)}, f32[8,128,128]{2,1,0:T(8,128)S(1)}, f32[8,128,128]{2,1,0:T(8,128)S(1)}, s32[]{:T(128)}, ...), condition=%wide.region_47.48_spmd.clone, body=%wide.region_46.47_spmd.clone.sunk | while | flops 201850880 | bytes 3670135 | solution.py:137
  636.1 7.4 collective-permute-start.3
  648.0 6.2 collective-permute-start.3
  658.8 6.8 collective-permute-start.3
  670.2 6.8 collective-permute-start.3
  681.6 6.8 collective-permute-start.3
  693.7 7.1 collective-permute-start.3
  707.4 7.1 collective-permute-start.3
  714.5 6.3 collective-permute-done.3
  722.0 29.4 %while.147 = (s32[]{:T(128)}, f32[8,128,128]{2,1,0:T(8,128)S(1)}, f32[4,8,64,128]{3,2,1,0:T(8,128)}, f32[4,8,1,1]{1,3,2,0:T(1,128)S(1)}, f32[4,8,64,128]{3,2,1,0...) while((s32[]{:T(128)}, f32[8,128,128]{2,1,0:T(8,128)S(1)}, ...), condition=%wide.region_50.51_spmd, body=%wide.region_49.50_spmd.sunk | while | flops 352714752 | bytes 4984009 | solution.py:138
  766.1 43.5 %collective-permute-done.11 = bf16[1024,1024]{1,0:T(8,128)(2,1)S(1)} collective-permute-done((bf16[1024,1024]{1,0:T(8,128)(2,1)S(1)}, bf16[1024,1024]{1,0:T(8,128)(2,1)S(1)}, u32[]{:S(2)}, u32[]{:S(2)}) %collective-permute-start.11) | collective-permute-done | bytes 2097184 | tf_op jit(solution)/shard_map/ppermute | solution.py:26
  816.6 188.0 %reduce-scatter.2.cloned.1.call-done = bf16[32,1024]{1,0:T(8,128)(2,1)} async-done(((bf16[1024,1024]{1,0:T(8,128)(2,1)}), bf16[32,1024]{1,0:T(8,128)(2,1)}) %reduce-scatter.2.cloned.1.call-update) | async-done | bytes 65552 | tf_op jit(solution)/shard_map/reduce_scatter | solution.py:195
  (560 shorter events, 544.2 us)
Async XLA Ops:
  7.2 748.7 %copy-start = (bf16[1,1,256,1024]{3,2,1,0:T(8,128)(2,1)S(1)}, bf16[1,1,256,1024]{3,2,1,0:T(8,128)(2,1)}, u32[]{:S(2)}) copy-start(bf16[1,1,256,1024]{3,2,1,0:T(8,128)(2,1)} %param.55) | copy-start | bytes 1572868
  7.2 997.4 %reduce-scatter.2.cloned.1.call-start = ((), (), s32[]{:S(2)}) async-start(), calls=%async_computation.1 | async-start | bytes 2162688 | tf_op jit(solution)/shard_map/reduce_scatter | solution.py:195
  15.0 16.0 %copy-start.25 = (bf16[1,256,1024]{2,1,0:T(8,128)(2,1)}, bf16[1,256,1024]{2,1,0:T(8,128)(2,1)S(1)}, u32[]{:S(2)}) copy-start(bf16[1,256,1024]{2,1,0:T(8,128)(2,1)S(1)} %get-tuple-element.1072) | copy-start | bytes 1572868
  89.3 12.5 %collective-permute-start = (bf16[8,128,128]{2,1,0:T(8,128)(2,1)S(1)}, bf16[8,128,128]{2,1,0:T(8,128)(2,1)S(1)}, u32[]{:S(2)}, u32[]{:S(2)}) collective-permute-start(bf16[8,128,128]{2,1,0:T(8,128)(2,1)S(1)} %fusion.635), channel_id=1, source_target_pairs={{0,4},{4,8},{8,12},{12,16},{16,20},{20,24},{24,28},{1,5},{5,9},{9,... | collective-permute-start | bytes 786440 | tf_op jit(solution)/shard_map/while/body/eval_jaxpr/ppermute | solution.py:16
  102.5 11.6 %collective-permute-start = (bf16[8,128,128]{2,1,0:T(8,128)(2,1)S(1)}, bf16[8,128,128]{2,1,0:T(8,128)(2,1)S(1)}, u32[]{:S(2)}, u32[]{:S(2)}) collective-permute-start(bf16[8,128,128]{2,1,0:T(8,128)(2,1)S(1)} %fusion.635), channel_id=1, source_target_pairs={{0,4},{4,8},{8,12},{12,16},{16,20},{20,24},{24,28},{1,5},{5,9},{9,... | collective-permute-start | bytes 786440 | tf_op jit(solution)/shard_map/while/body/eval_jaxpr/ppermute | solution.py:16
  114.8 10.8 %collective-permute-start = (bf16[8,128,128]{2,1,0:T(8,128)(2,1)S(1)}, bf16[8,128,128]{2,1,0:T(8,128)(2,1)S(1)}, u32[]{:S(2)}, u32[]{:S(2)}) collective-permute-start(bf16[8,128,128]{2,1,0:T(8,128)(2,1)S(1)} %fusion.635), channel_id=1, source_target_pairs={{0,4},{4,8},{8,12},{12,16},{16,20},{20,24},{24,28},{1,5},{5,9},{9,... | collective-permute-start | bytes 786440 | tf_op jit(solution)/shard_map/while/body/eval_jaxpr/ppermute | solution.py:16
  126.3 9.9 collective-permute-start
  136.8 9.8 collective-permute-start
  147.3 10.0 collective-permute-start
  158.0 10.7 %collective-permute-start = (bf16[8,128,128]{2,1,0:T(8,128)(2,1)S(1)}, bf16[8,128,128]{2,1,0:T(8,128)(2,1)S(1)}, u32[]{:S(2)}, u32[]{:S(2)}) collective-permute-start(bf16[8,128,128]{2,1,0:T(8,128)(2,1)S(1)} %fusion.635), channel_id=1, source_target_pairs={{0,4},{4,8},{8,12},{12,16},{16,20},{20,24},{24,28},{1,5},{5,9},{9,... | collective-permute-start | bytes 786440 | tf_op jit(solution)/shard_map/while/body/eval_jaxpr/ppermute | solution.py:16
  200.4 6.3 collective-permute-start.4
  201.7 5.0 collective-permute-start.5
  264.1 10.7 %collective-permute-start.1 = (bf16[8,128,128]{2,1,0:T(8,128)(2,1)S(1)}, bf16[8,128,128]{2,1,0:T(8,128)(2,1)S(1)}, u32[]{:S(2)}, u32[]{:S(2)}) collective-permute-start(bf16[8,128,128]{2,1,0:T(8,128)(2,1)S(1)} %fusion.649), channel_id=1, source_target_pairs={{0,4},{4,8},{8,12},{12,16},{16,20},{20,24},{24,28},{1,5},{5,9},{9,... | collective-permute-start | bytes 786440 | tf_op jit(solution)/shard_map/while/body/eval_jaxpr/ppermute | solution.py:16
  275.5 10.7 %collective-permute-start.1 = (bf16[8,128,128]{2,1,0:T(8,128)(2,1)S(1)}, bf16[8,128,128]{2,1,0:T(8,128)(2,1)S(1)}, u32[]{:S(2)}, u32[]{:S(2)}) collective-permute-start(bf16[8,128,128]{2,1,0:T(8,128)(2,1)S(1)} %fusion.649), channel_id=1, source_target_pairs={{0,4},{4,8},{8,12},{12,16},{16,20},{20,24},{24,28},{1,5},{5,9},{9,... | collective-permute-start | bytes 786440 | tf_op jit(solution)/shard_map/while/body/eval_jaxpr/ppermute | solution.py:16
  286.9 10.7 %collective-permute-start.1 = (bf16[8,128,128]{2,1,0:T(8,128)(2,1)S(1)}, bf16[8,128,128]{2,1,0:T(8,128)(2,1)S(1)}, u32[]{:S(2)}, u32[]{:S(2)}) collective-permute-start(bf16[8,128,128]{2,1,0:T(8,128)(2,1)S(1)} %fusion.649), channel_id=1, source_target_pairs={{0,4},{4,8},{8,12},{12,16},{16,20},{20,24},{24,28},{1,5},{5,9},{9,... | collective-permute-start | bytes 786440 | tf_op jit(solution)/shard_map/while/body/eval_jaxpr/ppermute | solution.py:16
  298.3 11.4 %collective-permute-start.1 = (bf16[8,128,128]{2,1,0:T(8,128)(2,1)S(1)}, bf16[8,128,128]{2,1,0:T(8,128)(2,1)S(1)}, u32[]{:S(2)}, u32[]{:S(2)}) collective-permute-start(bf16[8,128,128]{2,1,0:T(8,128)(2,1)S(1)} %fusion.649), channel_id=1, source_target_pairs={{0,4},{4,8},{8,12},{12,16},{16,20},{20,24},{24,28},{1,5},{5,9},{9,... | collective-permute-start | bytes 786440 | tf_op jit(solution)/shard_map/while/body/eval_jaxpr/ppermute | solution.py:16
  310.3 12.8 %collective-permute-start.1 = (bf16[8,128,128]{2,1,0:T(8,128)(2,1)S(1)}, bf16[8,128,128]{2,1,0:T(8,128)(2,1)S(1)}, u32[]{:S(2)}, u32[]{:S(2)}) collective-permute-start(bf16[8,128,128]{2,1,0:T(8,128)(2,1)S(1)} %fusion.649), channel_id=1, source_target_pairs={{0,4},{4,8},{8,12},{12,16},{16,20},{20,24},{24,28},{1,5},{5,9},{9,... | collective-permute-start | bytes 786440 | tf_op jit(solution)/shard_map/while/body/eval_jaxpr/ppermute | solution.py:16
  323.8 13.6 %collective-permute-start.1 = (bf16[8,128,128]{2,1,0:T(8,128)(2,1)S(1)}, bf16[8,128,128]{2,1,0:T(8,128)(2,1)S(1)}, u32[]{:S(2)}, u32[]{:S(2)}) collective-permute-start(bf16[8,128,128]{2,1,0:T(8,128)(2,1)S(1)} %fusion.649), channel_id=1, source_target_pairs={{0,4},{4,8},{8,12},{12,16},{16,20},{20,24},{24,28},{1,5},{5,9},{9,... | collective-permute-start | bytes 786440 | tf_op jit(solution)/shard_map/while/body/eval_jaxpr/ppermute | solution.py:16
  338.1 11.9 %collective-permute-start.1 = (bf16[8,128,128]{2,1,0:T(8,128)(2,1)S(1)}, bf16[8,128,128]{2,1,0:T(8,128)(2,1)S(1)}, u32[]{:S(2)}, u32[]{:S(2)}) collective-permute-start(bf16[8,128,128]{2,1,0:T(8,128)(2,1)S(1)} %fusion.649), channel_id=1, source_target_pairs={{0,4},{4,8},{8,12},{12,16},{16,20},{20,24},{24,28},{1,5},{5,9},{9,... | collective-permute-start | bytes 786440 | tf_op jit(solution)/shard_map/while/body/eval_jaxpr/ppermute | solution.py:16
  380.3 6.5 collective-permute-start.6
  381.6 9.4 collective-permute-start.7
  386.7 6.5 copy-start.30
  448.4 11.3 %collective-permute-start.2 = (bf16[8,128,128]{2,1,0:T(8,128)(2,1)S(1)}, bf16[8,128,128]{2,1,0:T(8,128)(2,1)S(1)}, u32[]{:S(2)}, u32[]{:S(2)}) collective-permute-start(bf16[8,128,128]{2,1,0:T(8,128)(2,1)S(1)} %fusion.663), channel_id=1, source_target_pairs={{0,4},{4,8},{8,12},{12,16},{16,20},{20,24},{24,28},{1,5},{5,9},{9,... | collective-permute-start | bytes 786440 | tf_op jit(solution)/shard_map/while/body/eval_jaxpr/ppermute | solution.py:16
  460.4 10.1 collective-permute-start.2
  471.2 10.7 %collective-permute-start.2 = (bf16[8,128,128]{2,1,0:T(8,128)(2,1)S(1)}, bf16[8,128,128]{2,1,0:T(8,128)(2,1)S(1)}, u32[]{:S(2)}, u32[]{:S(2)}) collective-permute-start(bf16[8,128,128]{2,1,0:T(8,128)(2,1)S(1)} %fusion.663), channel_id=1, source_target_pairs={{0,4},{4,8},{8,12},{12,16},{16,20},{20,24},{24,28},{1,5},{5,9},{9,... | collective-permute-start | bytes 786440 | tf_op jit(solution)/shard_map/while/body/eval_jaxpr/ppermute | solution.py:16
  482.6 10.7 %collective-permute-start.2 = (bf16[8,128,128]{2,1,0:T(8,128)(2,1)S(1)}, bf16[8,128,128]{2,1,0:T(8,128)(2,1)S(1)}, u32[]{:S(2)}, u32[]{:S(2)}) collective-permute-start(bf16[8,128,128]{2,1,0:T(8,128)(2,1)S(1)} %fusion.663), channel_id=1, source_target_pairs={{0,4},{4,8},{8,12},{12,16},{16,20},{20,24},{24,28},{1,5},{5,9},{9,... | collective-permute-start | bytes 786440 | tf_op jit(solution)/shard_map/while/body/eval_jaxpr/ppermute | solution.py:16
  493.9 11.5 %collective-permute-start.2 = (bf16[8,128,128]{2,1,0:T(8,128)(2,1)S(1)}, bf16[8,128,128]{2,1,0:T(8,128)(2,1)S(1)}, u32[]{:S(2)}, u32[]{:S(2)}) collective-permute-start(bf16[8,128,128]{2,1,0:T(8,128)(2,1)S(1)} %fusion.663), channel_id=1, source_target_pairs={{0,4},{4,8},{8,12},{12,16},{16,20},{20,24},{24,28},{1,5},{5,9},{9,... | collective-permute-start | bytes 786440 | tf_op jit(solution)/shard_map/while/body/eval_jaxpr/ppermute | solution.py:16
  506.1 12.9 %collective-permute-start.2 = (bf16[8,128,128]{2,1,0:T(8,128)(2,1)S(1)}, bf16[8,128,128]{2,1,0:T(8,128)(2,1)S(1)}, u32[]{:S(2)}, u32[]{:S(2)}) collective-permute-start(bf16[8,128,128]{2,1,0:T(8,128)(2,1)S(1)} %fusion.663), channel_id=1, source_target_pairs={{0,4},{4,8},{8,12},{12,16},{16,20},{20,24},{24,28},{1,5},{5,9},{9,... | collective-permute-start | bytes 786440 | tf_op jit(solution)/shard_map/while/body/eval_jaxpr/ppermute | solution.py:16
  519.7 13.5 %collective-permute-start.2 = (bf16[8,128,128]{2,1,0:T(8,128)(2,1)S(1)}, bf16[8,128,128]{2,1,0:T(8,128)(2,1)S(1)}, u32[]{:S(2)}, u32[]{:S(2)}) collective-permute-start(bf16[8,128,128]{2,1,0:T(8,128)(2,1)S(1)} %fusion.663), channel_id=1, source_target_pairs={{0,4},{4,8},{8,12},{12,16},{16,20},{20,24},{24,28},{1,5},{5,9},{9,... | collective-permute-start | bytes 786440 | tf_op jit(solution)/shard_map/while/body/eval_jaxpr/ppermute | solution.py:16
  563.5 3.4 collective-permute-start.8
  565.2 10.8 %collective-permute-start.9 = (bf16[256,1024]{1,0:T(8,128)(2,1)}, bf16[256,1024]{1,0:T(8,128)(2,1)S(1)}, u32[]{:S(2)}, u32[]{:S(2)}) collective-permute-start(bf16[256,1024]{1,0:T(8,128)(2,1)} %fusion.179), channel_id=1, source_target_pairs={{32,0},{64,32},{96,64},{33,1},{65,33},{97,65},{34,2},{66,34},{98,6... | collective-permute-start | bytes 1572872 | tf_op jit(solution)/shard_map/ppermute | solution.py:16
  576.2 8.3 copy-start.34
  636.1 11.3 %collective-permute-start.3 = (bf16[8,128,128]{2,1,0:T(8,128)(2,1)S(1)}, bf16[8,128,128]{2,1,0:T(8,128)(2,1)S(1)}, u32[]{:S(2)}, u32[]{:S(2)}) collective-permute-start(bf16[8,128,128]{2,1,0:T(8,128)(2,1)S(1)} %fusion.677), channel_id=1, source_target_pairs={{0,4},{4,8},{8,12},{12,16},{16,20},{20,24},{24,28},{1,5},{5,9},{9,... | collective-permute-start | bytes 786440 | tf_op jit(solution)/shard_map/while/body/eval_jaxpr/ppermute | solution.py:16
  648.0 10.1 collective-permute-start.3
  658.8 10.7 %collective-permute-start.3 = (bf16[8,128,128]{2,1,0:T(8,128)(2,1)S(1)}, bf16[8,128,128]{2,1,0:T(8,128)(2,1)S(1)}, u32[]{:S(2)}, u32[]{:S(2)}) collective-permute-start(bf16[8,128,128]{2,1,0:T(8,128)(2,1)S(1)} %fusion.677), channel_id=1, source_target_pairs={{0,4},{4,8},{8,12},{12,16},{16,20},{20,24},{24,28},{1,5},{5,9},{9,... | collective-permute-start | bytes 786440 | tf_op jit(solution)/shard_map/while/body/eval_jaxpr/ppermute | solution.py:16
  670.2 10.7 %collective-permute-start.3 = (bf16[8,128,128]{2,1,0:T(8,128)(2,1)S(1)}, bf16[8,128,128]{2,1,0:T(8,128)(2,1)S(1)}, u32[]{:S(2)}, u32[]{:S(2)}) collective-permute-start(bf16[8,128,128]{2,1,0:T(8,128)(2,1)S(1)} %fusion.677), channel_id=1, source_target_pairs={{0,4},{4,8},{8,12},{12,16},{16,20},{20,24},{24,28},{1,5},{5,9},{9,... | collective-permute-start | bytes 786440 | tf_op jit(solution)/shard_map/while/body/eval_jaxpr/ppermute | solution.py:16
  681.6 11.5 %collective-permute-start.3 = (bf16[8,128,128]{2,1,0:T(8,128)(2,1)S(1)}, bf16[8,128,128]{2,1,0:T(8,128)(2,1)S(1)}, u32[]{:S(2)}, u32[]{:S(2)}) collective-permute-start(bf16[8,128,128]{2,1,0:T(8,128)(2,1)S(1)} %fusion.677), channel_id=1, source_target_pairs={{0,4},{4,8},{8,12},{12,16},{16,20},{20,24},{24,28},{1,5},{5,9},{9,... | collective-permute-start | bytes 786440 | tf_op jit(solution)/shard_map/while/body/eval_jaxpr/ppermute | solution.py:16
  693.7 12.9 %collective-permute-start.3 = (bf16[8,128,128]{2,1,0:T(8,128)(2,1)S(1)}, bf16[8,128,128]{2,1,0:T(8,128)(2,1)S(1)}, u32[]{:S(2)}, u32[]{:S(2)}) collective-permute-start(bf16[8,128,128]{2,1,0:T(8,128)(2,1)S(1)} %fusion.677), channel_id=1, source_target_pairs={{0,4},{4,8},{8,12},{12,16},{16,20},{20,24},{24,28},{1,5},{5,9},{9,... | collective-permute-start | bytes 786440 | tf_op jit(solution)/shard_map/while/body/eval_jaxpr/ppermute | solution.py:16
  707.4 13.5 %collective-permute-start.3 = (bf16[8,128,128]{2,1,0:T(8,128)(2,1)S(1)}, bf16[8,128,128]{2,1,0:T(8,128)(2,1)S(1)}, u32[]{:S(2)}, u32[]{:S(2)}) collective-permute-start(bf16[8,128,128]{2,1,0:T(8,128)(2,1)S(1)} %fusion.677), channel_id=1, source_target_pairs={{0,4},{4,8},{8,12},{12,16},{16,20},{20,24},{24,28},{1,5},{5,9},{9,... | collective-permute-start | bytes 786440 | tf_op jit(solution)/shard_map/while/body/eval_jaxpr/ppermute | solution.py:16
  722.0 31.0 %copy-start.16 = (f32[4,8,64,128]{3,2,1,0:T(8,128)S(1)}, f32[4,8,64,128]{3,2,1,0:T(8,128)}, u32[]{:S(2)}) copy-start(f32[4,8,64,128]{3,2,1,0:T(8,128)} %copy-done.15) | copy-start | bytes 3145732
  722.0 31.0 %copy-start.18 = (f32[4,8,64,128]{3,2,1,0:T(8,128)S(1)}, f32[4,8,64,128]{3,2,1,0:T(8,128)}, u32[]{:S(2)}) copy-start(f32[4,8,64,128]{3,2,1,0:T(8,128)} %copy-done.17) | copy-start | bytes 3145732
  722.0 31.0 %copy-start.41 = (f32[4,8,64]{2,1,0:T(8,128)S(1)}, f32[4,8,64]{2,1,0:T(8,128)}, u32[]{:S(2)}) copy-start(f32[4,8,64]{2,1,0:T(8,128)} %copy-done.40) | copy-start | bytes 24580
  755.5 9.4 copy-start.23
  755.5 8.1 copy-start.20
  756.6 8.7 copy-start.33
  756.7 4.2 collective-permute-start.10
  760.9 48.7 %collective-permute-start.11 = (bf16[1024,1024]{1,0:T(8,128)(2,1)S(1)}, bf16[1024,1024]{1,0:T(8,128)(2,1)S(1)}, u32[]{:S(2)}, u32[]{:S(2)}) collective-permute-start(bf16[1024,1024]{1,0:T(8,128)(2,1)S(1)} %collective-permute-done.10), channel_id=1, source_target_pairs={{0,64},{64,0},{32,96},{96,32},{1,65},{65,1},{33,97},{97,33},{2,66}... | collective-permute-start | bytes 6291464 | tf_op jit(solution)/shard_map/ppermute | solution.py:26
  766.1 45.7 %copy-start.24 = (bf16[4,64,8,128]{3,1,2,0:T(8,128)(2,1)S(1)}, bf16[4,64,8,128]{3,1,2,0:T(8,128)(2,1)}, u32[]{:S(2)}) copy-start(bf16[4,64,8,128]{3,1,2,0:T(8,128)(2,1)} %copy-done.23) | copy-start | bytes 1572868
  (30 other events, 93.1 us)
Sparse Core Ops, SparseCore 0:
  811.9 192.6 reduce-scatter.1
where the time goes:
time: 1020 us; the launch traced here: 1010 us
  waiting for transfers between devices  380 us (37%)
  matrix products  335 us (33%)
  starting transfers between devices  198 us (19%)
  local copies, waits for them, and re-layouts  50.4 us (5%)
  other arithmetic  29.1 us (3%)
  between operations  16.1 us (2%)
    ppermute x34, starting transfers between devices, shifted(): return lax.ppermute(value, axis, pairs)  195 us
    reduce_scatter x1, waiting for transfers between devices, per_device(): lax.psum_scatter((own_down + mirrored).astype(jnp.bfloat16), ('ctx', 'dp'...  188 us
    ppermute x34, waiting for transfers between devices, shifted(): return lax.ppermute(value, axis, pairs)  144 us
    ppermute x2, waiting for transfers between devices, swapped(): return lax.ppermute(block, axis, route)  47.7 us
    dot_general x60, matrix products, compose_maps(): return jnp.einsum('hde,hef->hdf', later_map, earlier_map, precision=EXACT)  39.1 us
    dot_general x16, matrix products, block_step(): jnp.einsum('hcd,hce->hde', key_tail, new_values, precision=EXACT)  32.9 us
    dot_general x16, matrix products, span_map(): jnp.einsum('hcd,hce->hde', key_tail, erase_rows, precision=EXACT)  32.7 us
    dot_general x16, matrix products, span_map(): jnp.einsum('hcd,hce->hde', key_tail, target_rows, precision=EXACT)  32.6 us
  transfers between devices with their start and end apart: 37, of which 34 were waited for; matrix products, arithmetic and copies ran while one was open for 1% of the time, Pallas kernels for 0%

commit v1 on v0

v1 whole, which is shorter than its diff:
```python
import functools

import jax
import jax.numpy as jnp
from jax import lax
from jax.experimental import pallas as pl
from jax.experimental.pallas import tpu as pltpu
from jax.sharding import PartitionSpec as P

MESH = pl.DeviceIdType.MESH
EPSILON = 1e-06
EXACT = lax.Precision.HIGHEST
BF = jnp.bfloat16
F32 = jnp.float32
HEADS = 8
DIM = 128
TOK = 256
WIDTH = 1024
CH = 4
COLS = WIDTH // CH
UNIT = 32
GROUP = 8


def mm(a, b):
    return jnp.dot(a, b, preferred_element_type=F32)


def mm_nt(a, b):
    return lax.dot_general(a, b, (((1,), (1,)), ((), ())), preferred_element_type=F32)


def level_mask(size):
    row = lax.broadcasted_iota(jnp.int32, (DIM, DIM), 0)
    col = lax.broadcasted_iota(jnp.int32, (DIM, DIM), 1)
    if size == 0:
        return (row == col).astype(F32)
    if size == DIM:
        return (row >= col).astype(F32)
    same = (row // (2 * size)) == (col // (2 * size))
    return (same & ((row // size) > (col // size))).astype(F32)


LEVELS = (1, 2, 4, 8, 16, 32, 64)


def block_inverses(parts, masks):
    eye = masks[0]
    results = [eye - a * masks[1] for a in parts]
    for level in range(2, 8):
        offs = [a * masks[level] for a in parts]
        inner = [mm(o, t).astype(BF) for o, t in zip(offs, results)]
        results = [t - mm(t, y).astype(BF) for t, y in zip(results, inner)]
    return results


def head_maps(heads, proj, rstd, beta, cum, cum_rows, masks, low, put):
    first, second = slice(0, DIM), slice(DIM, TOK)
    state = []
    for h in heads:
        q = proj[:, pl.ds(h * DIM, DIM)] * rstd
        k = proj[:, pl.ds(WIDTH + h * DIM, DIM)] * rstd
        v = proj[:, pl.ds(2 * WIDTH + h * DIM, DIM)] * rstd
        q = q * (lax.rsqrt(jnp.sum(q * q, axis=-1, keepdims=True) + EPSILON) * DIM ** -0.5)
        k = k * lax.rsqrt(jnp.sum(k * k, axis=-1, keepdims=True) + EPSILON)
        b = beta[:, h : h + 1]
        c = jnp.broadcast_to(cum[:, HEADS + h : HEADS + h + 1], (TOK, DIM))
        row = cum_rows[HEADS + h : HEADS + h + 1, :]
        growth = jnp.exp(c)
        last = c[TOK - 1 : TOK, :]
        qb, kb, kbeta = q.astype(BF), k.astype(BF), (k * b).astype(BF)
        d11 = jnp.exp(jnp.minimum(c[first] - row[:, first], 0.0))
        d21 = jnp.exp(jnp.minimum(c[second] - row[:, first], 0.0))
        d22 = jnp.exp(jnp.minimum(c[second] - row[:, second], 0.0))
        lhs = jnp.concatenate([kbeta, qb], axis=0)
        g1 = mm_nt(lhs, kb[first])
        g2 = mm_nt(jnp.concatenate([kbeta[second], qb[second]], axis=0), kb[second])
        a11 = (g1[0:128] * d11).astype(BF)
        a21 = (g1[128:256] * d21).astype(BF)
        s11 = (g1[256:384] * (d11 * low)).astype(BF)
        s21 = (g1[384:512] * d21).astype(BF)
        a22 = (g2[0:128] * d22).astype(BF)
        s22 = (g2[128:256] * (d22 * low)).astype(BF)
        rhs = jnp.concatenate([(k * (growth * b)).astype(BF), (v * b).astype(BF)], axis=1)
        tail = (k * jnp.exp(last - c)).T.astype(BF)
        state.append((a11, a22, a21, s11, s21, s22, rhs, tail, q * growth, jnp.exp(last)))
    inverses = block_inverses([s[0] for s in state] + [s[1] for s in state], masks)
    n = len(state)
    x1 = [mm(inverses[i], state[i][6][first]).astype(BF) for i in range(n)]
    r2 = [(state[i][6][second].astype(F32) - mm(state[i][2], x1[i])).astype(BF) for i in range(n)]
    x2 = [mm(inverses[n + i], r2[i]).astype(BF) for i in range(n)]
    for i, h in enumerate(heads):
        _, _, _, s11, s21, s22, _, tail, qg, fade = state[i]
        x = jnp.concatenate([x1[i], x2[i]], axis=0)
        z1 = mm(s11, x1[i])
        z2 = mm(jnp.concatenate([s21, s22], axis=1), x)
        kx = mm(tail, x)
        put(h, qg, z1, z2, kx, fade)


def kernel(
    dims,
    down_in, up_in, down_qkv, up_qkv, down_gates, up_gates, down_rates, up_rates,
    down_wo, up_wo, down_ct, up_ct,
    down_out, up_out, grad_out,
    wqkv, wo, wg, xbuf, ybuf, proj, hid, maskb, pmap, rmap, mmap, bmap, sin, sout,
    cot, ht, hg, part, gbuf, gsum,
    w_sem, wo_sem, x_recv, x_send, y_sem, s_recv, s_send, ct_recv, ct_send,
    h_recv, h_send, g_recv, g_send, go_sem,
):
    sections, spans, copies = dims
    p, c, d = lax.axis_index("pipe"), lax.axis_index("ctx"), lax.axis_index("dp")
    low_half = p < sections // 2
    share = WIDTH // (spans * copies)
    column = WIDTH // spans

    def is_down(t):
        return low_half == (t == 0)

    def at(pipe, ctx, dp):
        return (pipe, ctx, dp)

    def remote(src, dst, send, recv, where):
        return pltpu.make_async_remote_copy(
            src_ref=src, dst_ref=dst, send_sem=send, recv_sem=recv,
            device_id=where, device_id_type=MESH,
        )

    def weight_copy(t, n, qkv):
        rows = pl.ds(n * COLS, COLS)
        return pltpu.make_async_copy(qkv.at[0, rows], wqkv.at[t, rows], w_sem.at[t, n])

    def out_copy(t, out):
        return pltpu.make_async_copy(out.at[0], wo.at[t], wo_sem.at[t])

    def start_weights(t, qkv, out):
        for n in range(CH):
            weight_copy(t, n, qkv).start()
        out_copy(t, out).start()

    def input_copy(src, n):
        return pltpu.make_async_copy(
            src.at[0, :, pl.ds(n * COLS, COLS)], xbuf.at[0, n], x_recv.at[0, n]
        )

    @pl.when(p == 0)
    def _():
        for n in range(CH):
            input_copy(down_in, n).start()

    @pl.when(p == sections - 1)
    def _():
        for n in range(CH):
            input_copy(up_in, n).start()

    @pl.when(low_half)
    def _():
        start_weights(0, down_qkv, down_wo)
        start_weights(1, up_qkv, up_wo)

    @pl.when(jnp.logical_not(low_half))
    def _():
        start_weights(0, up_qkv, up_wo)
        start_weights(1, down_qkv, down_wo)

    barrier = pltpu.get_barrier_semaphore()
    mirror = sections - 1 - p
    pair = p + 1 - 2 * lax.rem(p, 2)
    peers = [at(pair, c, d), at(mirror, c, d)]
    for k in range(1, spans):
        other = lax.rem(c + k, spans)
        peers += [at(p, other, d), at(mirror, other, d)]
    for k in range(1, copies):
        peers.append(at(p, c, lax.rem(d + k, copies)))
    for peer in peers:
        pl.semaphore_signal(barrier, inc=1, device_id=peer, device_id_type=MESH)

    for level, size in enumerate((0,) + LEVELS + (DIM,)):
        maskb[level] = level_mask(size).astype(BF)
    for t in range(2):
        wg[t] = jnp.zeros_like(wg[t])
        wg[t, :, 0 : 2 * HEADS] = jnp.where(is_down(t), down_gates[0], up_gates[0])

    pl.semaphore_wait(barrier, len(peers))

    def cot_own(t, source):
        return pltpu.make_async_copy(source.at[0, 0], cot.at[t, d], ct_recv.at[t, d])

    def cot_copy(t, source, k):
        return remote(
            source.at[0, 0], cot.at[t, d], ct_send.at[t, k - 1], ct_recv.at[t, d],
            at(p, c, lax.rem(d + k, copies)),
        )

    def start_cot(t, source):
        cot_own(t, source).start()
        for k in range(1, copies):
            cot_copy(t, source, k).start()

    @pl.when(low_half)
    def _():
        start_cot(0, down_ct)
        start_cot(1, up_ct)

    @pl.when(jnp.logical_not(low_half))
    def _():
        start_cot(0, up_ct)
        start_cot(1, down_ct)

    def state_copy(t, h):
        return remote(
            sout.at[t, h], sin.at[t, h], s_send.at[t, h], s_recv.at[t, h],
            at(p, lax.rem(c + 1, spans), d),
        )

    def stage_of(t):
        early = jnp.where(low_half, p, sections - 1 - p)
        return jnp.where(t == 0, early, sections - 1 - early)

    def stream_copy(t, n):
        slot = jnp.where(stage_of(t) == 0, 0, 1)
        to = jnp.clip(jnp.where(is_down(t), p + 1, p - 1), 0, sections - 1)
        return remote(
            ybuf.at[t, n], xbuf.at[slot, n], x_send.at[t, n], x_recv.at[slot, n], at(to, c, d)
        )

    def result_copy(t, n, out):
        return pltpu.make_async_copy(
            ybuf.at[t, n], out.at[0, 0, :, pl.ds(n * COLS, COLS)], y_sem.at[t, n]
        )

    def hidden_own(t):
        return pltpu.make_async_copy(ht.at[t, d], hg.at[t, d], h_recv.at[t, d])

    def hidden_copy(t, k):
        to = lax.rem(d + k, copies)
        return remote(ht.at[t, to], hg.at[t, d], h_send.at[t, k - 1], h_recv.at[t, d], at(p, c, to))

    def grad_own(t):
        return pltpu.make_async_copy(part.at[t, c], gbuf.at[c], g_recv.at[c])

    def grad_copy(t, k):
        to = lax.rem(c + k, spans)
        slot = c + jnp.where(is_down(t), 0, spans)
        pipe = jnp.where(is_down(t), p, mirror)
        return remote(part.at[t, to], gbuf.at[slot], g_send.at[t, k], g_recv.at[slot], at(pipe, to, d))

    def section(t):
        square = jnp.zeros((TOK, 1), F32)
        logits = jnp.zeros((TOK, DIM), F32)
        for n in range(CH):
            pltpu.make_async_copy(xbuf.at[t, n], xbuf.at[t, n], x_recv.at[t, n]).wait()
            weight_copy(t, n, down_qkv).wait()
            x = xbuf[t, n]
            xf = x.astype(F32)
            square += jnp.sum(xf * xf, axis=-1, keepdims=True)
            logits += mm(x, wg[t, n * COLS : (n + 1) * COLS, :])
            for j in range(6):
                block = slice(512 * j, 512 * (j + 1))
                product = mm(x, wqkv[t, n * COLS : (n + 1) * COLS, block])
                if n == 0:
                    proj[:, block] = product
                else:
                    proj[:, block] += product
        rstd = lax.rsqrt(square * (1.0 / WIDTH) + EPSILON)
        logits = logits * rstd
        rates = jnp.where(is_down(t), down_rates[...], up_rates[...])
        rates = jnp.concatenate(
            [jnp.zeros((1, HEADS), F32), rates, jnp.zeros((1, DIM - 2 * HEADS), F32)], axis=1
        )
        beta = jax.nn.sigmoid(logits)
        log_decay = -rates * (jnp.maximum(logits, 0.0) + jnp.log1p(jnp.exp(-jnp.abs(logits))))
        row = lax.broadcasted_iota(jnp.int32, (TOK, TOK), 0)
        col = lax.broadcasted_iota(jnp.int32, (TOK, TOK), 1)
        cum = jnp.dot(
            (row >= col).astype(F32), log_decay, preferred_element_type=F32, precision=EXACT
        )
        cum_rows = cum.T
        masks = [maskb[level] for level in range(8)]
        low = maskb[8].astype(F32)
        eye = maskb[0].astype(F32)

        def put(h, qg, z1, z2, kx, fade):
            pmap[h, 0:DIM] = (qg[0:DIM] - z1[:, 0:DIM]).astype(BF)
            pmap[h, DIM:TOK] = (qg[DIM:TOK] - z2[:, 0:DIM]).astype(BF)
            rmap[h, 0:DIM] = z1[:, DIM:TOK]
            rmap[h, DIM:TOK] = z2[:, DIM:TOK]
            mmap[h] = (eye * fade - kx[:, 0:DIM]).astype(BF)
            bmap[h] = kx[:, DIM:TOK]

        for start in range(0, HEADS, GROUP):
            head_maps(
                range(start, start + GROUP), proj, rstd, beta, cum, cum_rows, masks, low, put
            )

        for h in range(HEADS):
            @pl.when(c == 0)
            def _():
                sin[t, h] = jnp.zeros((DIM, DIM), BF)

            @pl.when(c > 0)
            def _():
                state_copy(t, h).wait_recv()

            s = sin[t, h]
            sout[t, h] = (mm(mmap[h], s) + bmap[h]).astype(BF)

            @pl.when(c < spans - 1)
            def _():
                state_copy(t, h).start()

            o = mm(pmap[h], s) + rmap[h]
            o = o * lax.rsqrt(jnp.mean(o * o, axis=-1, keepdims=True) + EPSILON)
            hid[:, h * DIM : (h + 1) * DIM] = o.astype(BF)

        out_copy(t, down_wo).wait()
        for n in range(CH):
            block = slice(n * COLS, (n + 1) * COLS)
            y = xbuf[t, n].astype(F32) + mm(hid[...], wo[t, :, block])
            ybuf[t, n] = y.astype(BF)

            @pl.when(stage_of(t) < sections - 1)
            def _():
                stream_copy(t, n).start()

            @pl.when(is_down(t))
            def _():
                result_copy(t, n, down_out).start()

            @pl.when(jnp.logical_not(is_down(t)))
            def _():
                result_copy(t, n, up_out).start()

        for h in range(HEADS):
            flipped = hid[:, h * DIM : (h + 1) * DIM].T
            for u in range(DIM // UNIT):
                row0 = h * DIM + u * UNIT
                span, rest = row0 // column, row0 % column
                to, i = rest // share, rest % share
                ht[t, to, span * share + i : span * share + i + UNIT] = flipped[
                    u * UNIT : (u + 1) * UNIT
                ]
        hidden_own(t).start()
        for k in range(1, copies):
            hidden_copy(t, k).start()

    def gradient(t):
        for j in range(copies):
            pltpu.make_async_copy(cot.at[t, j], cot.at[t, j], ct_recv.at[t, j]).wait()
            pltpu.make_async_copy(hg.at[t, j], hg.at[t, j], h_recv.at[t, j]).wait()
        for n in range(CH):
            block = slice(n * COLS, (n + 1) * COLS)
            total = mm(hg[t, 0], cot[t, 0, :, block])
            for j in range(1, copies):
                total += mm(hg[t, j], cot[t, j, :, block])
            part[t, :, :, block] = total.astype(BF).reshape(spans, share, COLS)
        for k in range(1, spans):
            grad_copy(t, k).start()

        @pl.when(is_down(t))
        def _():
            grad_own(t).start()

        @pl.when(jnp.logical_not(is_down(t)))
        def _():
            grad_copy(t, 0).start()

    outer = (p == 0) | (p == sections - 1)

    def turn(i, carry):
        middle = jnp.where(outer, 2, 1)
        is_section = (i == 0) | (i == middle)

        @pl.when(is_section)
        def _():
            section(jnp.where(i == 0, 0, 1))

        @pl.when(jnp.logical_not(is_section))
        def _():
            gradient(jnp.where(i == 3, 1, 0))

        return carry

    lax.fori_loop(0, 4, turn, 0)

    for j in range(2 * spans):
        pltpu.make_async_copy(gbuf.at[j], gbuf.at[j], g_recv.at[j]).wait()
    total = gbuf[0].astype(F32)
    for j in range(1, 2 * spans):
        total += gbuf[j].astype(F32)
    gsum[...] = total
    final = pltpu.make_async_copy(gsum, grad_out.at[0], go_sem)
    final.start()

    for t in range(2):
        for n in range(CH):
            result_copy(t, n, down_out).wait()

            @pl.when(stage_of(t) < sections - 1)
            def _():
                stream_copy(t, n).wait_send()

        @pl.when(c < spans - 1)
        def _():
            for h in range(HEADS):
                state_copy(t, h).wait_send()

        for k in range(1, copies):
            cot_copy(t, down_ct, k).wait_send()
            hidden_copy(t, k).wait_send()
        for k in range(1, spans):
            grad_copy(t, k).wait_send()

        @pl.when(jnp.logical_not(is_down(t)))
        def _():
            grad_copy(t, 0).wait_send()

    final.wait()


def per_device(dims, *arrays):
    sections, spans, copies = dims
    share = WIDTH // (spans * copies)
    hbm = pl.BlockSpec(memory_space=pl.ANY)
    vmem = pl.BlockSpec(memory_space=pltpu.VMEM)
    dma = pltpu.SemaphoreType.DMA
    return pl.pallas_call(
        functools.partial(kernel, dims),
        out_shape=(
            jax.ShapeDtypeStruct((1, 1, TOK, WIDTH), BF),
            jax.ShapeDtypeStruct((1, 1, TOK, WIDTH), BF),
            jax.ShapeDtypeStruct((1, share, WIDTH), F32),
        ),
        in_specs=[hbm] * 4 + [vmem] * 4 + [hbm] * 4,
        out_specs=(hbm, hbm, hbm),
        scratch_shapes=[
            pltpu.VMEM((2, WIDTH, 3 * WIDTH), BF),
            pltpu.VMEM((2, WIDTH, WIDTH), BF),
            pltpu.VMEM((2, WIDTH, DIM), BF),
            pltpu.VMEM((2, CH, TOK, COLS), BF),
            pltpu.VMEM((2, CH, TOK, COLS), BF),
            pltpu.VMEM((TOK, 3 * WIDTH), F32),
            pltpu.VMEM((TOK, WIDTH), BF),
            pltpu.VMEM((9, DIM, DIM), BF),
            pltpu.VMEM((HEADS, TOK, DIM), BF),
            pltpu.VMEM((HEADS, TOK, DIM), F32),
            pltpu.VMEM((HEADS, DIM, DIM), BF),
            pltpu.VMEM((HEADS, DIM, DIM), F32),
            pltpu.VMEM((2, HEADS, DIM, DIM), BF),
            pltpu.VMEM((2, HEADS, DIM, DIM), BF),
            pltpu.VMEM((2, copies, TOK, WIDTH), BF),
            pltpu.VMEM((2, copies, spans * share, TOK), BF),
            pltpu.VMEM((2, copies, spans * share, TOK), BF),
            pltpu.VMEM((2, spans, share, WIDTH), BF),
            pltpu.VMEM((2 * spans, share, WIDTH), BF),
            pltpu.VMEM((share, WIDTH), F32),
            dma((2, CH)),
            dma((2,)),
            dma((2, CH)),
            dma((2, CH)),
            dma((2, CH)),
            dma((2, HEADS)),
            dma((2, HEADS)),
            dma((2, copies)),
            dma((2, copies)),
            dma((2, copies)),
            dma((2, copies)),
            dma((2 * spans,)),
            dma((2, spans)),
            dma,
        ],
        compiler_params=pltpu.CompilerParams(
            collective_id=0, has_side_effects=True, vmem_limit_bytes=60 * 1024 * 1024
        ),
    )(*arrays)


def solution(mesh):
    dims = (mesh.shape["pipe"], mesh.shape["ctx"], mesh.shape["dp"])
    return jax.shard_map(
        functools.partial(per_device, dims),
        mesh=mesh,
        in_specs=(
            P("dp", "ctx", None),
            P("dp", "ctx", None),
            P("pipe", None, None),
            P("pipe", None, None),
            P("pipe", None, None),
            P("pipe", None, None),
            P("pipe", None),
            P("pipe", None),
            P("pipe", None, None),
            P("pipe", None, None),
            P("pipe", "dp", "ctx", None),
            P("pipe", "dp", "ctx", None),
        ),
        out_specs=(
            P("pipe", "dp", "ctx", None),
            P("pipe", "dp", "ctx", None),
            P("pipe", ("ctx", "dp"), None),
        ),
        check_vma=False,
    )
```

time: 1020 us -> 127 us (0.12)
  the two profiles are of different devices: /device:TPU:0 before, /device:TPU:37 now
where the time goes in v1:
time: 127 us
  Pallas kernels  118 us (93%)
  local copies, waits for them, and re-layouts  8.5 us (7%)
    pallas_call x1, Pallas kernels, per_device(): pl.pallas_call(functools.partial(kernel, dims), out_shape=(jax.ShapeDtype...  118 us
    unnamed x5, local copies, waits for them, and re-layouts  8.5 us

profile of v1, /device:TPU:37, one launch (start us, length us, event | category | flops | bytes accessed | tf_op | source)
XLA Modules:
  0.0 126.9 jit_solution(7817803285069935059)
XLA Ops:
  0.6 1.6 %copy.15.down_gates = bf16[1,1024,16]{2,1,0:T(8,128)(2,1)} copy(bf16[1,1024,16]{1,2,0:T(8,128)(2,1)} %param.16) | data formatting | bytes 65536 | tf_op args[4]
  2.2 1.6 %copy.16.up_gates = bf16[1,1024,16]{2,1,0:T(8,128)(2,1)} copy(bf16[1,1024,16]{1,2,0:T(8,128)(2,1)} %param.17) | data formatting | bytes 65536 | tf_op args[5]
  3.8 117.7 %shard_map.139 = (bf16[1,1,256,1024]{3,2,1,0:T(8,128)(2,1)}, bf16[1,1,256,1024]{3,2,1,0:T(8,128)(2,1)}, f32[1,32,1024]{2,1,0:T(8,128)}) custom-call(bf16[1,256,1024]{2,1,0:T(8,128)(2,1)} %down_in.1, bf16[1,256,1024]{2,1,0:T(8,128)(2,1)} %up_in.1, bf16[1,1024,3072]{2,1,0:T(8,128)(2,1)} %down_qkv.1, bf16[1,1024,3072]{2,1,0:T(8,128)(2,1)} %up_qkv.1, ...), custom_call_target="tpu_custom_call" | custom-call | tf_op jit(solution)/shard_map/pallas_call | solution.py:427
  121.6 1.9 %copy.20 = bf16[1,1,256,1024]{3,2,1,0:T(8,128)(2,1)} copy(bf16[1,1,256,1024]{3,2,1,0:T(8,128)(2,1)} %get-tuple-element.6) | data formatting | bytes 1048576
  123.4 1.9 %copy.21 = bf16[1,1,256,1024]{3,2,1,0:T(8,128)(2,1)} copy(bf16[1,1,256,1024]{3,2,1,0:T(8,128)(2,1)} %get-tuple-element.7) | data formatting | bytes 1048576
  125.3 1.6 %copy.22 = f32[1,32,1024]{2,1,0:T(8,128)} copy(f32[1,32,1024]{2,1,0:T(8,128)} %get-tuple-element.8) | data formatting | bytes 262144

commit v2 on v1

--- a/solution.py
+++ b/solution.py
@@ -20,6 +20,8 @@
 COLS = WIDTH // CH
 UNIT = 32
 GROUP = 8
+PIECES = 2
+HANDS = 2
 
 
 def mm(a, b):
@@ -153,15 +155,16 @@
         for n in range(CH):
             input_copy(up_in, n).start()
 
-    @pl.when(low_half)
-    def _():
-        start_weights(0, down_qkv, down_wo)
-        start_weights(1, up_qkv, up_wo)
-
-    @pl.when(jnp.logical_not(low_half))
-    def _():
-        start_weights(0, up_qkv, up_wo)
-        start_weights(1, down_qkv, down_wo)
+    def load(t):
+        @pl.when(is_down(t))
+        def _():
+            start_weights(t, down_qkv, down_wo)
+
+        @pl.when(jnp.logical_not(is_down(t)))
+        def _():
+            start_weights(t, up_qkv, up_wo)
+
+    load(0)
 
     barrier = pltpu.get_barrier_semaphore()
     mirror = sections - 1 - p
@@ -178,10 +181,8 @@
     for level, size in enumerate((0,) + LEVELS + (DIM,)):
         maskb[level] = level_mask(size).astype(BF)
     for t in range(2):
-        wg[t] = jnp.zeros_like(wg[t])
-        wg[t, :, 0 : 2 * HEADS] = jnp.where(is_down(t), down_gates[0], up_gates[0])
-
-    pl.semaphore_wait(barrier, len(peers))
+        wg[t, 2 * HEADS :, :] = jnp.zeros((DIM - 2 * HEADS, WIDTH), BF)
+        wg[t, 0 : 2 * HEADS, :] = jnp.where(is_down(t), down_gates[0], up_gates[0])
 
     def cot_own(t, source):
         return pltpu.make_async_copy(source.at[0, 0], cot.at[t, d], ct_recv.at[t, d])
@@ -197,15 +198,24 @@
         for k in range(1, copies):
             cot_copy(t, source, k).start()
 
-    @pl.when(low_half)
+    def start_cots(t):
+        @pl.when(is_down(t))
+        def _():
+            start_cot(t, down_ct)
+
+        @pl.when(jnp.logical_not(is_down(t)))
+        def _():
+            start_cot(t, up_ct)
+
+    def meet():
+        pl.semaphore_wait(barrier, len(peers))
+        start_cots(0)
+
+    outer = (p == 0) | (p == sections - 1)
+
+    @pl.when(jnp.logical_not(outer))
     def _():
-        start_cot(0, down_ct)
-        start_cot(1, up_ct)
-
-    @pl.when(jnp.logical_not(low_half))
-    def _():
-        start_cot(0, up_ct)
-        start_cot(1, down_ct)
+        meet()
 
     def state_copy(t, h):
         return remote(
@@ -229,12 +239,19 @@
             ybuf.at[t, n], out.at[0, 0, :, pl.ds(n * COLS, COLS)], y_sem.at[t, n]
         )
 
-    def hidden_own(t):
-        return pltpu.make_async_copy(ht.at[t, d], hg.at[t, d], h_recv.at[t, d])
-
-    def hidden_copy(t, k):
+    def hidden_own(t, piece):
+        rows = pl.ds(piece * (spans * share // PIECES), spans * share // PIECES)
+        return pltpu.make_async_copy(
+            ht.at[t, d, rows], hg.at[t, d, rows], h_recv.at[t, d, piece]
+        )
+
+    def hidden_copy(t, k, piece):
         to = lax.rem(d + k, copies)
-        return remote(ht.at[t, to], hg.at[t, d], h_send.at[t, k - 1], h_recv.at[t, d], at(p, c, to))
+        rows = pl.ds(piece * (spans * share // PIECES), spans * share // PIECES)
+        return remote(
+            ht.at[t, to, rows], hg.at[t, d, rows], h_send.at[t, k - 1, piece],
+            h_recv.at[t, d, piece], at(p, c, to),
+        )
 
     def grad_own(t):
         return pltpu.make_async_copy(part.at[t, c], gbuf.at[c], g_recv.at[c])
@@ -245,6 +262,22 @@
         pipe = jnp.where(is_down(t), p, mirror)
         return remote(part.at[t, to], gbuf.at[slot], g_send.at[t, k], g_recv.at[slot], at(pipe, to, d))
 
+    def rates_of(t):
+        rates = jnp.where(is_down(t), down_rates[...], up_rates[...])
+        return jnp.concatenate(
+            [jnp.zeros((1, HEADS), F32), rates, jnp.zeros((1, DIM - 2 * HEADS), F32)], axis=1
+        )
+
+    def gate_values(logits, rates):
+        beta = jax.nn.sigmoid(logits)
+        log_decay = -rates * (jnp.maximum(logits, 0.0) + jnp.log1p(jnp.exp(-jnp.abs(logits))))
+        row = lax.broadcasted_iota(jnp.int32, (TOK, TOK), 0)
+        col = lax.broadcasted_iota(jnp.int32, (TOK, TOK), 1)
+        cum = jnp.dot(
+            (row >= col).astype(F32), log_decay, preferred_element_type=F32, precision=EXACT
+        )
+        return beta, cum, cum.T
+
     def section(t):
         square = jnp.zeros((TOK, 1), F32)
         logits = jnp.zeros((TOK, DIM), F32)
@@ -254,7 +287,10 @@
             x = xbuf[t, n]
             xf = x.astype(F32)
             square += jnp.sum(xf * xf, axis=-1, keepdims=True)
-            logits += mm(x, wg[t, n * COLS : (n + 1) * COLS, :])
+            logits += mm_nt(x, wg[t, :, n * COLS : (n + 1) * COLS])
+            if n == CH - 1:
+                rstd = lax.rsqrt(square * (1.0 / WIDTH) + EPSILON)
+                beta, cum, cum_rows = gate_values(logits * rstd, rates_of(t))
             for j in range(6):
                 block = slice(512 * j, 512 * (j + 1))
                 product = mm(x, wqkv[t, n * COLS : (n + 1) * COLS, block])
@@ -262,20 +298,11 @@
                     proj[:, block] = product
                 else:
                     proj[:, block] += product
-        rstd = lax.rsqrt(square * (1.0 / WIDTH) + EPSILON)
-        logits = logits * rstd
-        rates = jnp.where(is_down(t), down_rates[...], up_rates[...])
-        rates = jnp.concatenate(
-            [jnp.zeros((1, HEADS), F32), rates, jnp.zeros((1, DIM - 2 * HEADS), F32)], axis=1
-        )
-        beta = jax.nn.sigmoid(logits)
-        log_decay = -rates * (jnp.maximum(logits, 0.0) + jnp.log1p(jnp.exp(-jnp.abs(logits))))
-        row = lax.broadcasted_iota(jnp.int32, (TOK, TOK), 0)
-        col = lax.broadcasted_iota(jnp.int32, (TOK, TOK), 1)
-        cum = jnp.dot(
-            (row >= col).astype(F32), log_decay, preferred_element_type=F32, precision=EXACT
-        )
-        cum_rows = cum.T
+
+        @pl.when(t == 0)
+        def _():
+            load(1)
+
         masks = [maskb[level] for level in range(8)]
         low = maskb[8].astype(F32)
         eye = maskb[0].astype(F32)
@@ -293,6 +320,10 @@
                 range(start, start + GROUP), proj, rstd, beta, cum, cum_rows, masks, low, put
             )
 
+        @pl.when((t == 0) & outer)
+        def _():
+            meet()
+
         for h in range(HEADS):
             @pl.when(c == 0)
             def _():
@@ -311,28 +342,9 @@
 
             o = mm(pmap[h], s) + rmap[h]
             o = o * lax.rsqrt(jnp.mean(o * o, axis=-1, keepdims=True) + EPSILON)
-            hid[:, h * DIM : (h + 1) * DIM] = o.astype(BF)
-
-        out_copy(t, down_wo).wait()
-        for n in range(CH):
-            block = slice(n * COLS, (n + 1) * COLS)
-            y = xbuf[t, n].astype(F32) + mm(hid[...], wo[t, :, block])
-            ybuf[t, n] = y.astype(BF)
-
-            @pl.when(stage_of(t) < sections - 1)
-            def _():
-                stream_copy(t, n).start()
-
-            @pl.when(is_down(t))
-            def _():
-                result_copy(t, n, down_out).start()
-
-            @pl.when(jnp.logical_not(is_down(t)))
-            def _():
-                result_copy(t, n, up_out).start()
-
-        for h in range(HEADS):
-            flipped = hid[:, h * DIM : (h + 1) * DIM].T
+            o = o.astype(BF)
+            hid[:, h * DIM : (h + 1) * DIM] = o
+            flipped = o.T
             for u in range(DIM // UNIT):
                 row0 = h * DIM + u * UNIT
                 span, rest = row0 // column, row0 % column
@@ -340,14 +352,42 @@
                 ht[t, to, span * share + i : span * share + i + UNIT] = flipped[
                     u * UNIT : (u + 1) * UNIT
                 ]
-        hidden_own(t).start()
-        for k in range(1, copies):
-            hidden_copy(t, k).start()
+            if h % (HEADS // PIECES) == HEADS // PIECES - 1:
+                piece = h // (HEADS // PIECES)
+                hidden_own(t, piece).start()
+                for k in range(1, copies):
+                    hidden_copy(t, k, piece).start()
+
+        out_copy(t, down_wo).wait()
+        for n in range(CH):
+            block = slice(n * COLS, (n + 1) * COLS)
+            y = xbuf[t, n].astype(F32) + mm(hid[...], wo[t, :, block])
+            ybuf[t, n] = y.astype(BF)
+
+            @pl.when(stage_of(t) < sections - 1)
+            def _():
+                stream_copy(t, n).start()
+
+            @pl.when(is_down(t))
+            def _():
+                result_copy(t, n, down_out).start()
+
+            @pl.when(jnp.logical_not(is_down(t)))
+            def _():
+                result_copy(t, n, up_out).start()
+
+        @pl.when(t == 0)
+        def _():
+            start_cots(1)
 
     def gradient(t):
         for j in range(copies):
             pltpu.make_async_copy(cot.at[t, j], cot.at[t, j], ct_recv.at[t, j]).wait()
-            pltpu.make_async_copy(hg.at[t, j], hg.at[t, j], h_recv.at[t, j]).wait()
+            for piece in range(PIECES):
+                rows = pl.ds(piece * (spans * share // PIECES), spans * share // PIECES)
+                pltpu.make_async_copy(
+                    hg.at[t, j, rows], hg.at[t, j, rows], h_recv.at[t, j, piece]
+                ).wait()
         for n in range(CH):
             block = slice(n * COLS, (n + 1) * COLS)
             total = mm(hg[t, 0], cot[t, 0, :, block])
@@ -364,8 +404,6 @@
         @pl.when(jnp.logical_not(is_down(t)))
         def _():
             grad_copy(t, 0).start()
-
-    outer = (p == 0) | (p == sections - 1)
 
     def turn(i, carry):
         middle = jnp.where(outer, 2, 1)
@@ -407,7 +445,8 @@
 
         for k in range(1, copies):
             cot_copy(t, down_ct, k).wait_send()
-            hidden_copy(t, k).wait_send()
+            for piece in range(PIECES):
+                hidden_copy(t, k, piece).wait_send()
         for k in range(1, spans):
             grad_copy(t, k).wait_send()
 
@@ -416,6 +455,22 @@
             grad_copy(t, 0).wait_send()
 
     final.wait()
+
+
+def hand_over(down_in, up_in, grad_in, down_out, up_out, grad_out, sems):
+    rows = TOK // HANDS
+    moves = []
+    for i, (src, dst) in enumerate(((down_in, down_out), (up_in, up_out))):
+        for n in range(HANDS):
+            part = (0, 0, pl.ds(n * rows, rows))
+            moves.append(
+                pltpu.make_async_copy(src.at[part], dst.at[part], sems.at[i * HANDS + n])
+            )
+    moves.append(pltpu.make_async_copy(grad_in, grad_out, sems.at[2 * HANDS]))
+    for move in moves:
+        move.start()
+    for move in moves:
+        move.wait()
 
 
 def per_device(dims, *arrays):
@@ -424,7 +479,7 @@
     hbm = pl.BlockSpec(memory_space=pl.ANY)
     vmem = pl.BlockSpec(memory_space=pltpu.VMEM)
     dma = pltpu.SemaphoreType.DMA
-    return pl.pallas_call(
+    down_acts, up_acts, grad = pl.pallas_call(
         functools.partial(kernel, dims),
         out_shape=(
             jax.ShapeDtypeStruct((1, 1, TOK, WIDTH), BF),
@@ -436,7 +491,7 @@
         scratch_shapes=[
             pltpu.VMEM((2, WIDTH, 3 * WIDTH), BF),
             pltpu.VMEM((2, WIDTH, WIDTH), BF),
-            pltpu.VMEM((2, WIDTH, DIM), BF),
+            pltpu.VMEM((2, DIM, WIDTH), BF),
             pltpu.VMEM((2, CH, TOK, COLS), BF),
             pltpu.VMEM((2, CH, TOK, COLS), BF),
             pltpu.VMEM((TOK, 3 * WIDTH), F32),
@@ -463,8 +518,8 @@
             dma((2, HEADS)),
             dma((2, copies)),
             dma((2, copies)),
-            dma((2, copies)),
-            dma((2, copies)),
+            dma((2, copies, PIECES)),
+            dma((2, copies, PIECES)),
             dma((2 * spans,)),
             dma((2, spans)),
             dma,
@@ -472,7 +527,14 @@
         compiler_params=pltpu.CompilerParams(
             collective_id=0, has_side_effects=True, vmem_limit_bytes=60 * 1024 * 1024
         ),
-    )(*arrays)
+    )(*arrays[:4], *(jnp.swapaxes(gates, 1, 2) for gates in arrays[4:6]), *arrays[6:])
+    return pl.pallas_call(
+        hand_over,
+        out_shape=tuple(jax.ShapeDtypeStruct(a.shape, a.dtype) for a in (down_acts, up_acts, grad)),
+        in_specs=[hbm] * 3,
+        out_specs=(hbm, hbm, hbm),
+        scratch_shapes=[dma((2 * HANDS + 1,))],
+    )(down_acts, up_acts, grad)
 
 
 def solution(mesh):

time: 127 us -> 142 us (1.12)
  Pallas kernels: 118 us -> 141 us
  local copies, waits for them, and re-layouts: 8.5 us -> 0 us
    pallas_call x0 -> x1, Pallas kernels: none -> 36.9 us  [per_device(): pl.pallas_call(hand_over, out_shape=tuple((jax.ShapeDtypeStruct(a.shape,...]
    pallas_call x1, Pallas kernels: 118 us -> 104 us  [per_device(): pl.pallas_call(functools.partial(kernel, dims), out_shape=(jax.ShapeDtype...]
    unnamed x5 -> x0, local copies, waits for them, and re-layouts: 8.5 us -> none
where the time goes in v2:
time: 142 us
  Pallas kernels  141 us (99%)
    pallas_call x1, Pallas kernels, per_device(): pl.pallas_call(functools.partial(kernel, dims), out_shape=(jax.ShapeDtype...  104 us
    pallas_call x1, Pallas kernels, per_device(): pl.pallas_call(hand_over, out_shape=tuple((jax.ShapeDtypeStruct(a.shape,...  36.9 us

profile of v2, /device:TPU:37, one launch (start us, length us, event | category | flops | bytes accessed | tf_op | source)
XLA Modules:
  0.0 141.8 jit_solution(12324718143903787005)
XLA Ops:
  0.6 104.3 %shard_map.139 = (bf16[1,1,256,1024]{3,2,1,0:T(8,128)(2,1)}, bf16[1,1,256,1024]{3,2,1,0:T(8,128)(2,1)}, f32[1,32,1024]{2,1,0:T(8,128)}) custom-call(bf16[1,256,1024]{2,1,0:T(8,128)(2,1)} %down_in.1, bf16[1,256,1024]{2,1,0:T(8,128)(2,1)} %up_in.1, bf16[1,1024,3072]{2,1,0:T(8,128)(2,1)} %down_qkv.1, bf16[1,1024,3072]{2,1,0:T(8,128)(2,1)} %up_qkv.1, ...), custom_call_target="tpu_custom_call" | custom-call | tf_op jit(solution)/shard_map/pallas_call | solution.py:482
  104.9 36.9 %shard_map.140 = (bf16[1,1,256,1024]{3,2,1,0:T(8,128)(2,1)}, bf16[1,1,256,1024]{3,2,1,0:T(8,128)(2,1)}, f32[1,32,1024]{2,1,0:T(8,128)}) custom-call(bf16[1,1,256,1024]{3,2,1,0:T(8,128)(2,1)} %get-tuple-element.6.down_in, bf16[1,1,256,1024]{3,2,1,0:T(8,128)(2,1)} %get-tuple-element.7.up_in, f32[1,32,1024]{2,1,0:T(8,128)} %get-tuple-element.8.grad_in), custom_call_target="tpu_custom_call" | custom-call | tf_op jit(solution)/shard_map/pallas_call | solution.py:531

commit v3 on v2

--- a/solution.py
+++ b/solution.py
@@ -457,20 +457,24 @@
     final.wait()
 
 
-def hand_over(down_in, up_in, grad_in, down_out, up_out, grad_out, sems):
+def hand_over(down_in, up_in, grad_in, down_out, up_out, grad_out, acts, grad, in_sems, out_sems):
     rows = TOK // HANDS
     moves = []
     for i, (src, dst) in enumerate(((down_in, down_out), (up_in, up_out))):
         for n in range(HANDS):
             part = (0, 0, pl.ds(n * rows, rows))
-            moves.append(
-                pltpu.make_async_copy(src.at[part], dst.at[part], sems.at[i * HANDS + n])
-            )
-    moves.append(pltpu.make_async_copy(grad_in, grad_out, sems.at[2 * HANDS]))
-    for move in moves:
-        move.start()
-    for move in moves:
-        move.wait()
+            moves.append((src.at[part], acts.at[i, pl.ds(n * rows, rows)], dst.at[part]))
+    moves.append((grad_in.at[0], grad, grad_out.at[0]))
+    loads, stores = [], []
+    for i, (src, here, dst) in enumerate(moves):
+        loads.append(pltpu.make_async_copy(src, here, in_sems.at[i]))
+        stores.append(pltpu.make_async_copy(here, dst, out_sems.at[i]))
+        loads[i].start()
+    for load, store in zip(loads, stores):
+        load.wait()
+        store.start()
+    for store in stores:
+        store.wait()
 
 
 def per_device(dims, *arrays):
@@ -533,7 +537,12 @@
         out_shape=tuple(jax.ShapeDtypeStruct(a.shape, a.dtype) for a in (down_acts, up_acts, grad)),
         in_specs=[hbm] * 3,
         out_specs=(hbm, hbm, hbm),
-        scratch_shapes=[dma((2 * HANDS + 1,))],
+        scratch_shapes=[
+            pltpu.VMEM((2, TOK, WIDTH), BF),
+            pltpu.VMEM((share, WIDTH), F32),
+            dma((2 * HANDS + 1,)),
+            dma((2 * HANDS + 1,)),
+        ],
     )(down_acts, up_acts, grad)
 
 

time: 142 us -> 107 us (0.75)
  Pallas kernels: 141 us -> 106 us
    pallas_call x1, Pallas kernels: 36.9 us -> 2.04 us  [per_device(): pl.pallas_call(hand_over, out_shape=tuple((jax.ShapeDtypeStruct(a.shape,...]
where the time goes in v3:
time: 107 us
  Pallas kernels  106 us (99%)
    pallas_call x1, Pallas kernels, per_device(): pl.pallas_call(functools.partial(kernel, dims), out_shape=(jax.ShapeDtype...  104 us

profile of v3, /device:TPU:37, one launch (start us, length us, event | category | flops | bytes accessed | tf_op | source)
XLA Modules:
  0.0 106.9 jit_solution(12033442197594317841)
XLA Ops:
  0.6 104.3 %shard_map.139 = (bf16[1,1,256,1024]{3,2,1,0:T(8,128)(2,1)}, bf16[1,1,256,1024]{3,2,1,0:T(8,128)(2,1)}, f32[1,32,1024]{2,1,0:T(8,128)}) custom-call(bf16[1,256,1024]{2,1,0:T(8,128)(2,1)} %down_in.1, bf16[1,256,1024]{2,1,0:T(8,128)(2,1)} %up_in.1, bf16[1,1024,3072]{2,1,0:T(8,128)(2,1)} %down_qkv.1, bf16[1,1024,3072]{2,1,0:T(8,128)(2,1)} %up_qkv.1, ...), custom_call_target="tpu_custom_call" | custom-call | tf_op jit(solution)/shard_map/pallas_call | solution.py:486
  104.9 2.0 %shard_map.140 = (bf16[1,1,256,1024]{3,2,1,0:T(8,128)(2,1)}, bf16[1,1,256,1024]{3,2,1,0:T(8,128)(2,1)}, f32[1,32,1024]{2,1,0:T(8,128)}) custom-call(bf16[1,1,256,1024]{3,2,1,0:T(8,128)(2,1)} %get-tuple-element.6.down_in, bf16[1,1,256,1024]{3,2,1,0:T(8,128)(2,1)} %get-tuple-element.7.up_in, f32[1,32,1024]{2,1,0:T(8,128)} %get-tuple-element.8.grad_in), custom_call_target="tpu_custom_call" | custom-call | tf_op jit(solution)/shard_map/pallas_call | solution.py:535

commit v4 on v3

--- a/solution.py
+++ b/solution.py
@@ -19,8 +19,8 @@
 CH = 4
 COLS = WIDTH // CH
 UNIT = 32
-GROUP = 8
-PIECES = 2
+PIECES = 4
+CHAIN = ((0, 1, 2, 3), (4, 5), (6, 7))
 HANDS = 2
 
 
@@ -56,48 +56,69 @@
     return results
 
 
-def head_maps(heads, proj, rstd, beta, cum, cum_rows, masks, low, put):
+def decay_of(gap):
+    return jnp.exp(jnp.minimum(gap, 0.0)).astype(BF)
+
+
+def lane_of(compact, lane):
+    return jnp.broadcast_to(compact[:, lane : lane + 1], (TOK, DIM))
+
+
+def head_maps(heads, proj, rstd, power, beta, cum, select, masks, low, eye, put):
     first, second = slice(0, DIM), slice(DIM, TOK)
+    lanes = lax.broadcasted_iota(jnp.int32, (TOK, DIM), 1)
+    tail = jnp.exp(cum[TOK - 1 : TOK, :] - cum)
+    fade = jnp.exp(cum[TOK - 1 : TOK, :])
+    rows = jnp.where(lanes < HEADS, beta, cum).T
+    brows = rows.astype(BF)
+    tail_rows = tail.T
+
+    def square_sums(start):
+        raw = proj[:, start : start + WIDTH]
+        return mm((raw * raw).astype(BF), select)
+
+    floor = (EPSILON * DIM) * (square_sums(0) + EPSILON * power)
+    nk = rstd * lax.rsqrt(square_sums(WIDTH) * (rstd * rstd) + EPSILON)
+    rstd_all = jnp.broadcast_to(rstd, (TOK, DIM))
     state = []
     for h in heads:
-        q = proj[:, pl.ds(h * DIM, DIM)] * rstd
-        k = proj[:, pl.ds(WIDTH + h * DIM, DIM)] * rstd
-        v = proj[:, pl.ds(2 * WIDTH + h * DIM, DIM)] * rstd
-        q = q * (lax.rsqrt(jnp.sum(q * q, axis=-1, keepdims=True) + EPSILON) * DIM ** -0.5)
-        k = k * lax.rsqrt(jnp.sum(k * k, axis=-1, keepdims=True) + EPSILON)
-        b = beta[:, h : h + 1]
-        c = jnp.broadcast_to(cum[:, HEADS + h : HEADS + h + 1], (TOK, DIM))
-        row = cum_rows[HEADS + h : HEADS + h + 1, :]
+        lane = HEADS + h
+        q = proj[:, h * DIM : (h + 1) * DIM]
+        k = proj[:, WIDTH + h * DIM : WIDTH + (h + 1) * DIM] * lane_of(nk, lane)
+        v = proj[:, 2 * WIDTH + h * DIM : 2 * WIDTH + (h + 1) * DIM]
+        c = lane_of(cum, lane)
         growth = jnp.exp(c)
-        last = c[TOK - 1 : TOK, :]
-        qb, kb, kbeta = q.astype(BF), k.astype(BF), (k * b).astype(BF)
-        d11 = jnp.exp(jnp.minimum(c[first] - row[:, first], 0.0))
-        d21 = jnp.exp(jnp.minimum(c[second] - row[:, first], 0.0))
-        d22 = jnp.exp(jnp.minimum(c[second] - row[:, second], 0.0))
-        lhs = jnp.concatenate([kbeta, qb], axis=0)
-        g1 = mm_nt(lhs, kb[first])
-        g2 = mm_nt(jnp.concatenate([kbeta[second], qb[second]], axis=0), kb[second])
-        a11 = (g1[0:128] * d11).astype(BF)
-        a21 = (g1[128:256] * d21).astype(BF)
-        s11 = (g1[256:384] * (d11 * low)).astype(BF)
-        s21 = (g1[384:512] * d21).astype(BF)
-        a22 = (g2[0:128] * d22).astype(BF)
-        s22 = (g2[128:256] * (d22 * low)).astype(BF)
-        rhs = jnp.concatenate([(k * (growth * b)).astype(BF), (v * b).astype(BF)], axis=1)
-        tail = (k * jnp.exp(last - c)).T.astype(BF)
-        state.append((a11, a22, a21, s11, s21, s22, rhs, tail, q * growth, jnp.exp(last)))
+        qb, kb = q.astype(BF), k.astype(BF)
+        rhs = jnp.concatenate([(k * growth).astype(BF), (v * rstd_all).astype(BF)], axis=1)
+        weight = (tail_rows[lane : lane + 1, :] * rows[h : h + 1, :]).astype(BF)
+        flipped = kb.T * weight
+        qg = q * growth
+        crow, brow = rows[lane : lane + 1, :], brows[h : h + 1, :]
+        d11 = decay_of(c[first] - crow[:, first]) * brow[:, first]
+        d21 = decay_of(c[second] - crow[:, first]) * brow[:, first]
+        d22 = decay_of(c[second] - crow[:, second]) * brow[:, second]
+        g1 = mm_nt(jnp.concatenate([kb, qb], axis=0), kb[first]).astype(BF)
+        g2 = mm_nt(jnp.concatenate([kb[second], qb[second]], axis=0), kb[second]).astype(BF)
+        a11 = g1[0:128] * d11
+        a21 = g1[128:256] * d21
+        s11 = g1[256:384] * (d11 * low)
+        s21 = g1[384:512] * d21
+        a22 = g2[0:128] * d22
+        s22 = g2[128:256] * (d22 * low)
+        state.append((a11, a22, a21, s11, s21, s22, rhs, flipped, qg))
     inverses = block_inverses([s[0] for s in state] + [s[1] for s in state], masks)
     n = len(state)
     x1 = [mm(inverses[i], state[i][6][first]).astype(BF) for i in range(n)]
-    r2 = [(state[i][6][second].astype(F32) - mm(state[i][2], x1[i])).astype(BF) for i in range(n)]
+    r2 = [state[i][6][second] - mm(state[i][2], x1[i]).astype(BF) for i in range(n)]
     x2 = [mm(inverses[n + i], r2[i]).astype(BF) for i in range(n)]
     for i, h in enumerate(heads):
-        _, _, _, s11, s21, s22, _, tail, qg, fade = state[i]
+        _, _, _, s11, s21, s22, _, flipped, qg = state[i]
         x = jnp.concatenate([x1[i], x2[i]], axis=0)
         z1 = mm(s11, x1[i])
         z2 = mm(jnp.concatenate([s21, s22], axis=1), x)
-        kx = mm(tail, x)
-        put(h, qg, z1, z2, kx, fade)
+        kx = mm(flipped, x)
+        put(h, qg, z1, z2, kx, eye * fade[:, HEADS + h : HEADS + h + 1])
+    return floor
 
 
 def kernel(
@@ -105,7 +126,7 @@
     down_in, up_in, down_qkv, up_qkv, down_gates, up_gates, down_rates, up_rates,
     down_wo, up_wo, down_ct, up_ct,
     down_out, up_out, grad_out,
-    wqkv, wo, wg, xbuf, ybuf, proj, hid, maskb, pmap, rmap, mmap, bmap, sin, sout,
+    wqkv, wo, wg, xbuf, ybuf, proj, hid, maskb, select, floor, pmap, rmap, mmap, bmap, sin, sout,
     cot, ht, hg, part, gbuf, gsum,
     w_sem, wo_sem, x_recv, x_send, y_sem, s_recv, s_send, ct_recv, ct_send,
     h_recv, h_send, g_recv, g_send, go_sem,
@@ -180,6 +201,9 @@
 
     for level, size in enumerate((0,) + LEVELS + (DIM,)):
         maskb[level] = level_mask(size).astype(BF)
+    for h in range(HEADS):
+        lanes = lax.broadcasted_iota(jnp.int32, (DIM, DIM), 1)
+        select[h * DIM : (h + 1) * DIM] = (lanes == HEADS + h).astype(F32).astype(BF)
     for t in range(2):
         wg[t, 2 * HEADS :, :] = jnp.zeros((DIM - 2 * HEADS, WIDTH), BF)
         wg[t, 0 : 2 * HEADS, :] = jnp.where(is_down(t), down_gates[0], up_gates[0])
@@ -253,14 +277,18 @@
             h_recv.at[t, d, piece], at(p, c, to),
         )
 
-    def grad_own(t):
-        return pltpu.make_async_copy(part.at[t, c], gbuf.at[c], g_recv.at[c])
-
-    def grad_copy(t, k):
-        to = lax.rem(c + k, spans)
+    def grad_own(t, to):
+        return pltpu.make_async_copy(part.at[t, to], gbuf.at[to], g_recv.at[to])
+
+    def grad_copy(t, to):
         slot = c + jnp.where(is_down(t), 0, spans)
         pipe = jnp.where(is_down(t), p, mirror)
-        return remote(part.at[t, to], gbuf.at[slot], g_send.at[t, k], g_recv.at[slot], at(pipe, to, d))
+        return remote(
+            part.at[t, to], gbuf.at[slot], g_send.at[t, to], g_recv.at[slot], at(pipe, to, d)
+        )
+
+    def stays(t, to):
+        return (c == to) & is_down(t)
 
     def rates_of(t):
         rates = jnp.where(is_down(t), down_rates[...], up_rates[...])
@@ -276,7 +304,7 @@
         cum = jnp.dot(
             (row >= col).astype(F32), log_decay, preferred_element_type=F32, precision=EXACT
         )
-        return beta, cum, cum.T
+        return beta, cum
 
     def section(t):
         square = jnp.zeros((TOK, 1), F32)
@@ -289,8 +317,9 @@
             square += jnp.sum(xf * xf, axis=-1, keepdims=True)
             logits += mm_nt(x, wg[t, :, n * COLS : (n + 1) * COLS])
             if n == CH - 1:
-                rstd = lax.rsqrt(square * (1.0 / WIDTH) + EPSILON)
-                beta, cum, cum_rows = gate_values(logits * rstd, rates_of(t))
+                power = square * (1.0 / WIDTH) + EPSILON
+                rstd = lax.rsqrt(power)
+                beta, cum = gate_values(logits * rstd, rates_of(t))
             for j in range(6):
                 block = slice(512 * j, 512 * (j + 1))
                 product = mm(x, wqkv[t, n * COLS : (n + 1) * COLS, block])
@@ -304,7 +333,7 @@
             load(1)
 
         masks = [maskb[level] for level in range(8)]
-        low = maskb[8].astype(F32)
+        low = maskb[8]
         eye = maskb[0].astype(F32)
 
         def put(h, qg, z1, z2, kx, fade):
@@ -312,51 +341,55 @@
             pmap[h, DIM:TOK] = (qg[DIM:TOK] - z2[:, 0:DIM]).astype(BF)
             rmap[h, 0:DIM] = z1[:, DIM:TOK]
             rmap[h, DIM:TOK] = z2[:, DIM:TOK]
-            mmap[h] = (eye * fade - kx[:, 0:DIM]).astype(BF)
+            mmap[h] = (fade - kx[:, 0:DIM]).astype(BF)
             bmap[h] = kx[:, DIM:TOK]
 
-        for start in range(0, HEADS, GROUP):
-            head_maps(
-                range(start, start + GROUP), proj, rstd, beta, cum, cum_rows, masks, low, put
-            )
+        floor[...] = head_maps(
+            range(HEADS), proj, rstd, power, beta, cum, select[...], masks, low, eye, put
+        )
 
         @pl.when((t == 0) & outer)
         def _():
             meet()
 
-        for h in range(HEADS):
-            @pl.when(c == 0)
-            def _():
+        @pl.when(c == 0)
+        def _():
+            for h in range(HEADS):
+                sout[t, h] = bmap[h].astype(BF)
+                state_copy(t, h).start()
                 sin[t, h] = jnp.zeros((DIM, DIM), BF)
 
+        for group in CHAIN:
             @pl.when(c > 0)
             def _():
-                state_copy(t, h).wait_recv()
-
-            s = sin[t, h]
-            sout[t, h] = (mm(mmap[h], s) + bmap[h]).astype(BF)
-
-            @pl.when(c < spans - 1)
-            def _():
-                state_copy(t, h).start()
-
-            o = mm(pmap[h], s) + rmap[h]
-            o = o * lax.rsqrt(jnp.mean(o * o, axis=-1, keepdims=True) + EPSILON)
-            o = o.astype(BF)
-            hid[:, h * DIM : (h + 1) * DIM] = o
-            flipped = o.T
-            for u in range(DIM // UNIT):
-                row0 = h * DIM + u * UNIT
-                span, rest = row0 // column, row0 % column
-                to, i = rest // share, rest % share
-                ht[t, to, span * share + i : span * share + i + UNIT] = flipped[
-                    u * UNIT : (u + 1) * UNIT
-                ]
-            if h % (HEADS // PIECES) == HEADS // PIECES - 1:
-                piece = h // (HEADS // PIECES)
-                hidden_own(t, piece).start()
-                for k in range(1, copies):
-                    hidden_copy(t, k, piece).start()
+                for h in group:
+                    state_copy(t, h).wait_recv()
+
+                    @pl.when(c < spans - 1)
+                    def _():
+                        sout[t, h] = (mm(mmap[h], sin[t, h]) + bmap[h]).astype(BF)
+                        state_copy(t, h).start()
+
+            for h in group:
+                o = mm(pmap[h], sin[t, h]) + rmap[h]
+                level = jnp.mean(o * o, axis=-1, keepdims=True)
+                o = o * lax.rsqrt(level + floor[:, HEADS + h : HEADS + h + 1])
+                o = o.astype(BF)
+                hid[:, h * DIM : (h + 1) * DIM] = o
+                flipped = o.T
+                for u in range(DIM // UNIT):
+                    row0 = h * DIM + u * UNIT
+                    span, rest = row0 // column, row0 % column
+                    to, i = rest // share, rest % share
+                    ht[t, to, span * share + i : span * share + i + UNIT] = flipped[
+                        u * UNIT : (u + 1) * UNIT
+                    ]
+            for piece in range(PIECES):
+                last = HEADS // PIECES * (piece + 1) - 1 if spans == HEADS else HEADS - 1
+                if last in group:
+                    hidden_own(t, piece).start()
+                    for k in range(1, copies):
+                        hidden_copy(t, k, piece).start()
 
         out_copy(t, down_wo).wait()
         for n in range(CH):
@@ -383,27 +416,28 @@
     def gradient(t):
         for j in range(copies):
             pltpu.make_async_copy(cot.at[t, j], cot.at[t, j], ct_recv.at[t, j]).wait()
-            for piece in range(PIECES):
-                rows = pl.ds(piece * (spans * share // PIECES), spans * share // PIECES)
+        size = spans * share // PIECES
+        for piece in range(PIECES):
+            rows = pl.ds(piece * size, size)
+            for j in range(copies):
                 pltpu.make_async_copy(
                     hg.at[t, j, rows], hg.at[t, j, rows], h_recv.at[t, j, piece]
                 ).wait()
-        for n in range(CH):
-            block = slice(n * COLS, (n + 1) * COLS)
-            total = mm(hg[t, 0], cot[t, 0, :, block])
+            total = mm(hg[t, 0, piece * size : (piece + 1) * size], cot[t, 0])
             for j in range(1, copies):
-                total += mm(hg[t, j], cot[t, j, :, block])
-            part[t, :, :, block] = total.astype(BF).reshape(spans, share, COLS)
-        for k in range(1, spans):
-            grad_copy(t, k).start()
-
-        @pl.when(is_down(t))
-        def _():
-            grad_own(t).start()
-
-        @pl.when(jnp.logical_not(is_down(t)))
-        def _():
-            grad_copy(t, 0).start()
+                total += mm(hg[t, j, piece * size : (piece + 1) * size], cot[t, j])
+            total = total.astype(BF)
+            for row0 in range(0, size, UNIT):
+                to, at_row = divmod(piece * size + row0, share)
+                part[t, to, at_row : at_row + UNIT] = total[row0 : row0 + UNIT]
+                if at_row + UNIT == share:
+                    @pl.when(stays(t, to))
+                    def _():
+                        grad_own(t, to).start()
+
+                    @pl.when(jnp.logical_not(stays(t, to)))
+                    def _():
+                        grad_copy(t, to).start()
 
     def turn(i, carry):
         middle = jnp.where(outer, 2, 1)
@@ -447,12 +481,10 @@
             cot_copy(t, down_ct, k).wait_send()
             for piece in range(PIECES):
                 hidden_copy(t, k, piece).wait_send()
-        for k in range(1, spans):
-            grad_copy(t, k).wait_send()
-
-        @pl.when(jnp.logical_not(is_down(t)))
-        def _():
-            grad_copy(t, 0).wait_send()
+        for to in range(spans):
+            @pl.when(jnp.logical_not(stays(t, to)))
+            def _():
+                grad_copy(t, to).wait_send()
 
     final.wait()
 
@@ -501,6 +533,8 @@
             pltpu.VMEM((TOK, 3 * WIDTH), F32),
             pltpu.VMEM((TOK, WIDTH), BF),
             pltpu.VMEM((9, DIM, DIM), BF),
+            pltpu.VMEM((WIDTH, DIM), BF),
+            pltpu.VMEM((TOK, DIM), F32),
             pltpu.VMEM((HEADS, TOK, DIM), BF),
             pltpu.VMEM((HEADS, TOK, DIM), F32),
             pltpu.VMEM((HEADS, DIM, DIM), BF),

time: 107 us -> 103 us (0.963)
  Pallas kernels: 106 us -> 102 us
    pallas_call x1, Pallas kernels: 104 us -> 100 us  [per_device(): pl.pallas_call(functools.partial(kernel, dims), out_shape=(jax.ShapeDtype...]
where the time goes in v4:
time: 103 us
  Pallas kernels  102 us (99%)
    pallas_call x1, Pallas kernels, per_device(): pl.pallas_call(functools.partial(kernel, dims), out_shape=(jax.ShapeDtype...  100 us

profile of v4, /device:TPU:37, one launch (start us, length us, event | category | flops | bytes accessed | tf_op | source)
XLA Modules:
  0.0 102.7 jit_solution(2958677753791665130)
XLA Ops:
  0.6 100.0 %shard_map.139 = (bf16[1,1,256,1024]{3,2,1,0:T(8,128)(2,1)}, bf16[1,1,256,1024]{3,2,1,0:T(8,128)(2,1)}, f32[1,32,1024]{2,1,0:T(8,128)}) custom-call(bf16[1,256,1024]{2,1,0:T(8,128)(2,1)} %down_in.1, bf16[1,256,1024]{2,1,0:T(8,128)(2,1)} %up_in.1, bf16[1,1024,3072]{2,1,0:T(8,128)(2,1)} %down_qkv.1, bf16[1,1024,3072]{2,1,0:T(8,128)(2,1)} %up_qkv.1, ...), custom_call_target="tpu_custom_call" | custom-call | tf_op jit(solution)/shard_map/pallas_call | solution.py:518
  100.6 2.0 %shard_map.140 = (bf16[1,1,256,1024]{3,2,1,0:T(8,128)(2,1)}, bf16[1,1,256,1024]{3,2,1,0:T(8,128)(2,1)}, f32[1,32,1024]{2,1,0:T(8,128)}) custom-call(bf16[1,1,256,1024]{3,2,1,0:T(8,128)(2,1)} %get-tuple-element.6.down_in, bf16[1,1,256,1024]{3,2,1,0:T(8,128)(2,1)} %get-tuple-element.7.up_in, f32[1,32,1024]{2,1,0:T(8,128)} %get-tuple-element.8.grad_in), custom_call_target="tpu_custom_call" | custom-call | tf_op jit(solution)/shard_map/pallas_call | solution.py:569

commit v5 on v4

--- a/solution.py
+++ b/solution.py
@@ -20,7 +20,6 @@
 COLS = WIDTH // CH
 UNIT = 32
 PIECES = 4
-CHAIN = ((0, 1, 2, 3), (4, 5), (6, 7))
 HANDS = 2
 
 
@@ -32,28 +31,35 @@
     return lax.dot_general(a, b, (((1,), (1,)), ((), ())), preferred_element_type=F32)
 
 
-def level_mask(size):
+def band_mask(inner, outer):
     row = lax.broadcasted_iota(jnp.int32, (DIM, DIM), 0)
     col = lax.broadcasted_iota(jnp.int32, (DIM, DIM), 1)
-    if size == 0:
+    if outer == 1:
         return (row == col).astype(F32)
-    if size == DIM:
+    if inner == 0:
         return (row >= col).astype(F32)
-    same = (row // (2 * size)) == (col // (2 * size))
-    return (same & ((row // size) > (col // size))).astype(F32)
-
-
-LEVELS = (1, 2, 4, 8, 16, 32, 64)
+    same = (row // outer) == (col // outer)
+    return (same & ((row // inner) > (col // inner))).astype(F32)
+
+
+MASKS = ((1, 1), (1, 8), (8, 64), (64, 128), (0, 128))
+
+
+def eightfold(starts, powers):
+    squares = [mm(n, n).astype(BF) for n in powers]
+    halves = [t + mm(n, t).astype(BF) for t, n in zip(starts, squares)]
+    fourths = [mm(n, n).astype(BF) for n in squares]
+    return [t + mm(n, t).astype(BF) for t, n in zip(halves, fourths)]
 
 
 def block_inverses(parts, masks):
-    eye = masks[0]
-    results = [eye - a * masks[1] for a in parts]
-    for level in range(2, 8):
-        offs = [a * masks[level] for a in parts]
-        inner = [mm(o, t).astype(BF) for o, t in zip(offs, results)]
-        results = [t - mm(t, y).astype(BF) for t, y in zip(results, inner)]
-    return results
+    inner = [a * masks[1] for a in parts]
+    results = eightfold([masks[0] - a for a in inner], inner)
+    steps = [mm(t, a * masks[2]).astype(BF) for t, a in zip(results, parts)]
+    results = [t - mm(n, t).astype(BF) for t, n in zip(results, steps)]
+    results = eightfold(results, steps)
+    steps = [mm(a * masks[3], t).astype(BF) for t, a in zip(results, parts)]
+    return [t - mm(t, y).astype(BF) for t, y in zip(results, steps)]
 
 
 def decay_of(gap):
@@ -126,10 +132,10 @@
     down_in, up_in, down_qkv, up_qkv, down_gates, up_gates, down_rates, up_rates,
     down_wo, up_wo, down_ct, up_ct,
     down_out, up_out, grad_out,
-    wqkv, wo, wg, xbuf, ybuf, proj, hid, maskb, select, floor, pmap, rmap, mmap, bmap, sin, sout,
+    wqkv, wo, wg, xbuf, ybuf, proj, hid, obuf, maskb, select, floor, pmap, rmap, mmap, bmap, bsend, sin, sout,
     cot, ht, hg, part, gbuf, gsum,
     w_sem, wo_sem, x_recv, x_send, y_sem, s_recv, s_send, ct_recv, ct_send,
-    h_recv, h_send, g_recv, g_send, go_sem,
+    ct_own, h_recv, h_send, g_recv, g_send, go_sem,
 ):
     sections, spans, copies = dims
     p, c, d = lax.axis_index("pipe"), lax.axis_index("ctx"), lax.axis_index("dp")
@@ -199,8 +205,8 @@
     for peer in peers:
         pl.semaphore_signal(barrier, inc=1, device_id=peer, device_id_type=MESH)
 
-    for level, size in enumerate((0,) + LEVELS + (DIM,)):
-        maskb[level] = level_mask(size).astype(BF)
+    for level, (inner, outer_size) in enumerate(MASKS):
+        maskb[level] = band_mask(inner, outer_size).astype(BF)
     for h in range(HEADS):
         lanes = lax.broadcasted_iota(jnp.int32, (DIM, DIM), 1)
         select[h * DIM : (h + 1) * DIM] = (lanes == HEADS + h).astype(F32).astype(BF)
@@ -208,19 +214,43 @@
         wg[t, 2 * HEADS :, :] = jnp.zeros((DIM - 2 * HEADS, WIDTH), BF)
         wg[t, 0 : 2 * HEADS, :] = jnp.where(is_down(t), down_gates[0], up_gates[0])
 
+    half = TOK // 2
+    before, after = lax.rem(d + copies - 1, copies), lax.rem(d + 1, copies)
+    ways = ((0, after),) if copies == 2 else ((0, after), (1, before))
+
     def cot_own(t, source):
-        return pltpu.make_async_copy(source.at[0, 0], cot.at[t, d], ct_recv.at[t, d])
-
-    def cot_copy(t, source, k):
+        return pltpu.make_async_copy(source.at[0, 0], cot.at[t, d], ct_own.at[t])
+
+    def cot_copy(t, source, way, to):
         return remote(
-            source.at[0, 0], cot.at[t, d], ct_send.at[t, k - 1], ct_recv.at[t, d],
-            at(p, c, lax.rem(d + k, copies)),
+            source.at[0, 0], cot.at[t, d], ct_send.at[t, way], ct_recv.at[t, way], at(p, c, to)
+        )
+
+    def cot_relay(t, way, to):
+        owner = before if way == 0 else after
+        part_rows = pl.ds(way * half, half)
+        return remote(
+            cot.at[t, owner, part_rows], cot.at[t, owner, part_rows], ct_send.at[t, 2 + way],
+            ct_recv.at[t, 2 + way], at(p, c, to),
         )
 
     def start_cot(t, source):
         cot_own(t, source).start()
-        for k in range(1, copies):
-            cot_copy(t, source, k).start()
+        for way, to in ways:
+            cot_copy(t, source, way, to).start()
+
+    def relay_cots(t):
+        for way, to in ways:
+            cot_copy(t, down_ct, way, to).wait_recv()
+        if copies == 4:
+            for way, to in ways:
+                cot_relay(t, way, to).start()
+
+    def wait_cots(t):
+        cot_own(t, down_ct).wait()
+        if copies == 4:
+            for way, to in ways:
+                cot_relay(t, way, to).wait_recv()
 
     def start_cots(t):
         @pl.when(is_down(t))
@@ -235,6 +265,10 @@
         pl.semaphore_wait(barrier, len(peers))
         start_cots(0)
 
+        @pl.when(jnp.logical_not(outer))
+        def _():
+            start_cots(1)
+
     outer = (p == 0) | (p == sections - 1)
 
     @pl.when(jnp.logical_not(outer))
@@ -244,6 +278,12 @@
     def state_copy(t, h):
         return remote(
             sout.at[t, h], sin.at[t, h], s_send.at[t, h], s_recv.at[t, h],
+            at(p, lax.rem(c + 1, spans), d),
+        )
+
+    def first_copy(t, h):
+        return remote(
+            bsend.at[t, h], sin.at[t, h], s_send.at[t, h], s_recv.at[t, h],
             at(p, lax.rem(c + 1, spans), d),
         )
 
@@ -332,8 +372,8 @@
         def _():
             load(1)
 
-        masks = [maskb[level] for level in range(8)]
-        low = maskb[8]
+        masks = [maskb[level] for level in range(4)]
+        low = maskb[4]
         eye = maskb[0].astype(F32)
 
         def put(h, qg, z1, z2, kx, fade):
@@ -343,6 +383,7 @@
             rmap[h, DIM:TOK] = z2[:, DIM:TOK]
             mmap[h] = (fade - kx[:, 0:DIM]).astype(BF)
             bmap[h] = kx[:, DIM:TOK]
+            bsend[t, h] = kx[:, DIM:TOK].astype(BF)
 
         floor[...] = head_maps(
             range(HEADS), proj, rstd, power, beta, cum, select[...], masks, low, eye, put
@@ -355,41 +396,51 @@
         @pl.when(c == 0)
         def _():
             for h in range(HEADS):
-                sout[t, h] = bmap[h].astype(BF)
-                state_copy(t, h).start()
+                first_copy(t, h).start()
                 sin[t, h] = jnp.zeros((DIM, DIM), BF)
 
-        for group in CHAIN:
-            @pl.when(c > 0)
-            def _():
-                for h in group:
-                    state_copy(t, h).wait_recv()
-
-                    @pl.when(c < spans - 1)
-                    def _():
-                        sout[t, h] = (mm(mmap[h], sin[t, h]) + bmap[h]).astype(BF)
-                        state_copy(t, h).start()
-
-            for h in group:
-                o = mm(pmap[h], sin[t, h]) + rmap[h]
-                level = jnp.mean(o * o, axis=-1, keepdims=True)
-                o = o * lax.rsqrt(level + floor[:, HEADS + h : HEADS + h + 1])
-                o = o.astype(BF)
-                hid[:, h * DIM : (h + 1) * DIM] = o
-                flipped = o.T
-                for u in range(DIM // UNIT):
-                    row0 = h * DIM + u * UNIT
-                    span, rest = row0 // column, row0 % column
-                    to, i = rest // share, rest % share
-                    ht[t, to, span * share + i : span * share + i + UNIT] = flipped[
-                        u * UNIT : (u + 1) * UNIT
-                    ]
+        def finish_head(h):
+            o = obuf[h % 2]
+            level = jnp.mean(o * o, axis=-1, keepdims=True)
+            o = o * lax.rsqrt(level + floor[:, HEADS + h : HEADS + h + 1])
+            o = o.astype(BF)
+            hid[:, h * DIM : (h + 1) * DIM] = o
+            flipped = o.T
+            for u in range(DIM // UNIT):
+                row0 = h * DIM + u * UNIT
+                span, rest = row0 // column, row0 % column
+                to, i = rest // share, rest % share
+                ht[t, to, span * share + i : span * share + i + UNIT] = flipped[
+                    u * UNIT : (u + 1) * UNIT
+                ]
+
+        def send_pieces(h):
             for piece in range(PIECES):
                 last = HEADS // PIECES * (piece + 1) - 1 if spans == HEADS else HEADS - 1
-                if last in group:
+                if last == h:
                     hidden_own(t, piece).start()
                     for k in range(1, copies):
                         hidden_copy(t, k, piece).start()
+
+        for h in range(HEADS):
+            @pl.when(c > 0)
+            def _():
+                state_copy(t, h).wait_recv()
+
+            s = sin[t, h]
+            sout[t, h] = (mm(mmap[h], s) + bmap[h]).astype(BF)
+            obuf[h % 2] = mm(pmap[h], s) + rmap[h]
+            if h > 0:
+                finish_head(h - 1)
+
+            @pl.when((c > 0) & (c < spans - 1))
+            def _():
+                state_copy(t, h).start()
+
+            if h > 0:
+                send_pieces(h - 1)
+        finish_head(HEADS - 1)
+        send_pieces(HEADS - 1)
 
         out_copy(t, down_wo).wait()
         for n in range(CH):
@@ -411,11 +462,18 @@
 
         @pl.when(t == 0)
         def _():
-            start_cots(1)
+            relay_cots(0)
+
+            @pl.when(outer)
+            def _():
+                start_cots(1)
+
+            @pl.when(jnp.logical_not(outer))
+            def _():
+                relay_cots(1)
 
     def gradient(t):
-        for j in range(copies):
-            pltpu.make_async_copy(cot.at[t, j], cot.at[t, j], ct_recv.at[t, j]).wait()
+        wait_cots(t)
         size = spans * share // PIECES
         for piece in range(PIECES):
             rows = pl.ds(piece * size, size)
@@ -451,6 +509,10 @@
         def _():
             gradient(jnp.where(i == 3, 1, 0))
 
+            @pl.when(outer & (i == 1))
+            def _():
+                relay_cots(1)
+
         return carry
 
     lax.fori_loop(0, 4, turn, 0)
@@ -477,8 +539,11 @@
             for h in range(HEADS):
                 state_copy(t, h).wait_send()
 
+        for way, to in ways:
+            cot_copy(t, down_ct, way, to).wait_send()
+            if copies == 4:
+                cot_relay(t, way, to).wait_send()
         for k in range(1, copies):
-            cot_copy(t, down_ct, k).wait_send()
             for piece in range(PIECES):
                 hidden_copy(t, k, piece).wait_send()
         for to in range(spans):
@@ -532,13 +597,15 @@
             pltpu.VMEM((2, CH, TOK, COLS), BF),
             pltpu.VMEM((TOK, 3 * WIDTH), F32),
             pltpu.VMEM((TOK, WIDTH), BF),
-            pltpu.VMEM((9, DIM, DIM), BF),
+            pltpu.VMEM((2, TOK, DIM), F32),
+            pltpu.VMEM((len(MASKS), DIM, DIM), BF),
             pltpu.VMEM((WIDTH, DIM), BF),
             pltpu.VMEM((TOK, DIM), F32),
             pltpu.VMEM((HEADS, TOK, DIM), BF),
             pltpu.VMEM((HEADS, TOK, DIM), F32),
             pltpu.VMEM((HEADS, DIM, DIM), BF),
             pltpu.VMEM((HEADS, DIM, DIM), F32),
+            pltpu.VMEM((2, HEADS, DIM, DIM), BF),
             pltpu.VMEM((2, HEADS, DIM, DIM), BF),
             pltpu.VMEM((2, HEADS, DIM, DIM), BF),
             pltpu.VMEM((2, copies, TOK, WIDTH), BF),
@@ -554,8 +621,9 @@
             dma((2, CH)),
             dma((2, HEADS)),
             dma((2, HEADS)),
-            dma((2, copies)),
-            dma((2, copies)),
+            dma((2, 4)),
+            dma((2, 4)),
+            dma((2,)),
             dma((2, copies, PIECES)),
             dma((2, copies, PIECES)),
             dma((2 * spans,)),

time: 103 us -> 101 us (0.981)
  Pallas kernels: 102 us -> 100 us
    pallas_call x1, Pallas kernels: 100 us -> 98 us  [per_device(): pl.pallas_call(functools.partial(kernel, dims), out_shape=(jax.ShapeDtype...]
where the time goes in v5:
time: 101 us
  Pallas kernels  100 us (99%)
    pallas_call x1, Pallas kernels, per_device(): pl.pallas_call(functools.partial(kernel, dims), out_shape=(jax.ShapeDtype...  98 us
    pallas_call x1, Pallas kernels, per_device(): pl.pallas_call(hand_over, out_shape=tuple((jax.ShapeDtypeStruct(a.shape,...  2.04 us

profile of v5, /device:TPU:37, one launch (start us, length us, event | category | flops | bytes accessed | tf_op | source)
XLA Modules:
  0.0 100.7 jit_solution(5437802591774734824)
XLA Ops:
  0.6 98.0 %shard_map.139 = (bf16[1,1,256,1024]{3,2,1,0:T(8,128)(2,1)}, bf16[1,1,256,1024]{3,2,1,0:T(8,128)(2,1)}, f32[1,32,1024]{2,1,0:T(8,128)}) custom-call(bf16[1,256,1024]{2,1,0:T(8,128)(2,1)} %down_in.1, bf16[1,256,1024]{2,1,0:T(8,128)(2,1)} %up_in.1, bf16[1,1024,3072]{2,1,0:T(8,128)(2,1)} %down_qkv.1, bf16[1,1024,3072]{2,1,0:T(8,128)(2,1)} %up_qkv.1, ...), custom_call_target="tpu_custom_call" | custom-call | tf_op jit(solution)/shard_map/pallas_call | solution.py:583
  98.6 2.0 %shard_map.140 = (bf16[1,1,256,1024]{3,2,1,0:T(8,128)(2,1)}, bf16[1,1,256,1024]{3,2,1,0:T(8,128)(2,1)}, f32[1,32,1024]{2,1,0:T(8,128)}) custom-call(bf16[1,1,256,1024]{3,2,1,0:T(8,128)(2,1)} %get-tuple-element.6.down_in, bf16[1,1,256,1024]{3,2,1,0:T(8,128)(2,1)} %get-tuple-element.7.up_in, f32[1,32,1024]{2,1,0:T(8,128)} %get-tuple-element.8.grad_in), custom_call_target="tpu_custom_call" | custom-call | tf_op jit(solution)/shard_map/pallas_call | solution.py:637

commit v6 on v5

--- a/solution.py
+++ b/solution.py
@@ -59,7 +59,8 @@
     results = [t - mm(n, t).astype(BF) for t, n in zip(results, steps)]
     results = eightfold(results, steps)
     steps = [mm(a * masks[3], t).astype(BF) for t, a in zip(results, parts)]
-    return [t - mm(t, y).astype(BF) for t, y in zip(results, steps)]
+    results = [t - mm(t, y).astype(BF) for t, y in zip(results, steps)]
+    return results
 
 
 def decay_of(gap):
@@ -70,36 +71,46 @@
     return jnp.broadcast_to(compact[:, lane : lane + 1], (TOK, DIM))
 
 
-def head_maps(heads, proj, rstd, power, beta, cum, select, masks, low, eye, put):
+def gate_rows(logits, rates, triangle):
+    row = lax.broadcasted_iota(jnp.int32, (2 * HEADS, TOK), 0)
+    decay = -rates * (jnp.maximum(logits, 0.0) + jnp.log1p(jnp.exp(-jnp.abs(logits))))
+    high = decay.astype(BF)
+    rest = decay - high.astype(F32)
+    middle = rest.astype(BF)
+    low = (rest - middle.astype(F32)).astype(BF)
+    sums = mm(jnp.concatenate([high, middle, low], axis=0), triangle)
+    total = sums[0:16] + sums[16:32] + sums[32:48]
+    return jnp.where(row < HEADS, jax.nn.sigmoid(logits), total)
+
+
+def head_maps(proj, power, gates, select, masks, low, eye, put):
     first, second = slice(0, DIM), slice(DIM, TOK)
-    lanes = lax.broadcasted_iota(jnp.int32, (TOK, DIM), 1)
-    tail = jnp.exp(cum[TOK - 1 : TOK, :] - cum)
-    fade = jnp.exp(cum[TOK - 1 : TOK, :])
-    rows = jnp.where(lanes < HEADS, beta, cum).T
-    brows = rows.astype(BF)
-    tail_rows = tail.T
+    rstd = lax.rsqrt(power)
+    columns = jnp.concatenate([gates, jnp.zeros((DIM - 2 * HEADS, TOK), F32)], axis=0).T
+    beta, cum = gates[0:HEADS], gates[HEADS : 2 * HEADS]
+    last = jnp.broadcast_to(cum[:, TOK - 1 : TOK], (HEADS, TOK))
+    weights = (beta * jnp.exp(last - cum)).astype(BF)
+    fades = jnp.exp(last[:, 0:DIM])
+    strengths = beta.astype(BF)
 
     def square_sums(start):
         raw = proj[:, start : start + WIDTH]
         return mm((raw * raw).astype(BF), select)
 
-    floor = (EPSILON * DIM) * (square_sums(0) + EPSILON * power)
     nk = rstd * lax.rsqrt(square_sums(WIDTH) * (rstd * rstd) + EPSILON)
-    rstd_all = jnp.broadcast_to(rstd, (TOK, DIM))
-    state = []
-    for h in heads:
+
+    def prepare(h):
         lane = HEADS + h
         q = proj[:, h * DIM : (h + 1) * DIM]
         k = proj[:, WIDTH + h * DIM : WIDTH + (h + 1) * DIM] * lane_of(nk, lane)
         v = proj[:, 2 * WIDTH + h * DIM : 2 * WIDTH + (h + 1) * DIM]
-        c = lane_of(cum, lane)
+        c = lane_of(columns, lane)
         growth = jnp.exp(c)
         qb, kb = q.astype(BF), k.astype(BF)
-        rhs = jnp.concatenate([(k * growth).astype(BF), (v * rstd_all).astype(BF)], axis=1)
-        weight = (tail_rows[lane : lane + 1, :] * rows[h : h + 1, :]).astype(BF)
-        flipped = kb.T * weight
+        rhs = jnp.concatenate([(k * growth).astype(BF), (v * rstd).astype(BF)], axis=1)
+        flipped = kb.T * weights[h : h + 1, :]
         qg = q * growth
-        crow, brow = rows[lane : lane + 1, :], brows[h : h + 1, :]
+        crow, brow = cum[h : h + 1, :], strengths[h : h + 1, :]
         d11 = decay_of(c[first] - crow[:, first]) * brow[:, first]
         d21 = decay_of(c[second] - crow[:, first]) * brow[:, first]
         d22 = decay_of(c[second] - crow[:, second]) * brow[:, second]
@@ -111,20 +122,25 @@
         s21 = g1[384:512] * d21
         a22 = g2[0:128] * d22
         s22 = g2[128:256] * (d22 * low)
-        state.append((a11, a22, a21, s11, s21, s22, rhs, flipped, qg))
-    inverses = block_inverses([s[0] for s in state] + [s[1] for s in state], masks)
-    n = len(state)
-    x1 = [mm(inverses[i], state[i][6][first]).astype(BF) for i in range(n)]
-    r2 = [state[i][6][second] - mm(state[i][2], x1[i]).astype(BF) for i in range(n)]
-    x2 = [mm(inverses[n + i], r2[i]).astype(BF) for i in range(n)]
-    for i, h in enumerate(heads):
-        _, _, _, s11, s21, s22, _, flipped, qg = state[i]
-        x = jnp.concatenate([x1[i], x2[i]], axis=0)
-        z1 = mm(s11, x1[i])
-        z2 = mm(jnp.concatenate([s21, s22], axis=1), x)
-        kx = mm(flipped, x)
-        put(h, qg, z1, z2, kx, eye * fade[:, HEADS + h : HEADS + h + 1])
-    return floor
+        return h, a11, a22, a21, s11, s21, s22, rhs, flipped, qg
+
+    def complete(state, inverses):
+        n = len(state)
+        x1 = [mm(inverses[i], state[i][7][first]).astype(BF) for i in range(n)]
+        r2 = [state[i][7][second] - mm(state[i][3], x1[i]).astype(BF) for i in range(n)]
+        x2 = [mm(inverses[n + i], r2[i]).astype(BF) for i in range(n)]
+        for i in range(n):
+            h, _, _, _, s11, s21, s22, _, flipped, qg = state[i]
+            x = jnp.concatenate([x1[i], x2[i]], axis=0)
+            z1 = mm(s11, x1[i])
+            z2 = mm(jnp.concatenate([s21, s22], axis=1), x)
+            kx = mm(flipped, x)
+            put(h, qg, z1, z2, kx, eye * fades[h : h + 1, :])
+
+    state = [prepare(h) for h in range(HEADS)]
+    inverses = block_inverses([s[1] for s in state] + [s[2] for s in state], masks)
+    complete(state, inverses)
+    return (EPSILON * DIM) * (square_sums(0) + EPSILON * power)
 
 
 def kernel(
@@ -132,7 +148,7 @@
     down_in, up_in, down_qkv, up_qkv, down_gates, up_gates, down_rates, up_rates,
     down_wo, up_wo, down_ct, up_ct,
     down_out, up_out, grad_out,
-    wqkv, wo, wg, xbuf, ybuf, proj, hid, obuf, maskb, select, floor, pmap, rmap, mmap, bmap, bsend, sin, sout,
+    wqkv, wo, wg, rates, triangle, xbuf, ybuf, proj, hid, obuf, maskb, select, floor, pmap, rmap, mmap, bmap, bsend, sin, sout,
     cot, ht, hg, part, gbuf, gsum,
     w_sem, wo_sem, x_recv, x_send, y_sem, s_recv, s_send, ct_recv, ct_send,
     ct_own, h_recv, h_send, g_recv, g_send, go_sem,
@@ -211,8 +227,16 @@
         lanes = lax.broadcasted_iota(jnp.int32, (DIM, DIM), 1)
         select[h * DIM : (h + 1) * DIM] = (lanes == HEADS + h).astype(F32).astype(BF)
     for t in range(2):
-        wg[t, 2 * HEADS :, :] = jnp.zeros((DIM - 2 * HEADS, WIDTH), BF)
-        wg[t, 0 : 2 * HEADS, :] = jnp.where(is_down(t), down_gates[0], up_gates[0])
+        wg[t] = jnp.where(is_down(t), down_gates[0], up_gates[0])
+        rate = jnp.where(is_down(t), down_rates[...], up_rates[...])
+        rate = jnp.concatenate(
+            [jnp.zeros((1, HEADS), F32), rate, jnp.zeros((1, DIM - 2 * HEADS), F32)], axis=1
+        )
+        rate = jnp.broadcast_to(rate, (TOK, DIM)).T
+        rates[t] = rate[0 : 2 * HEADS]
+    token = lax.broadcasted_iota(jnp.int32, (TOK, TOK), 0)
+    until = lax.broadcasted_iota(jnp.int32, (TOK, TOK), 1)
+    triangle[...] = (token <= until).astype(F32).astype(BF)
 
     half = TOK // 2
     before, after = lax.rem(d + copies - 1, copies), lax.rem(d + 1, copies)
@@ -330,36 +354,21 @@
     def stays(t, to):
         return (c == to) & is_down(t)
 
-    def rates_of(t):
-        rates = jnp.where(is_down(t), down_rates[...], up_rates[...])
-        return jnp.concatenate(
-            [jnp.zeros((1, HEADS), F32), rates, jnp.zeros((1, DIM - 2 * HEADS), F32)], axis=1
-        )
-
-    def gate_values(logits, rates):
-        beta = jax.nn.sigmoid(logits)
-        log_decay = -rates * (jnp.maximum(logits, 0.0) + jnp.log1p(jnp.exp(-jnp.abs(logits))))
-        row = lax.broadcasted_iota(jnp.int32, (TOK, TOK), 0)
-        col = lax.broadcasted_iota(jnp.int32, (TOK, TOK), 1)
-        cum = jnp.dot(
-            (row >= col).astype(F32), log_decay, preferred_element_type=F32, precision=EXACT
-        )
-        return beta, cum
-
     def section(t):
-        square = jnp.zeros((TOK, 1), F32)
-        logits = jnp.zeros((TOK, DIM), F32)
+        ones = jnp.ones((COLS, DIM), BF)
+        square = jnp.zeros((TOK, DIM), F32)
+        square_row = jnp.zeros((2 * HEADS, TOK), F32)
+        logits = jnp.zeros((2 * HEADS, TOK), F32)
         for n in range(CH):
             pltpu.make_async_copy(xbuf.at[t, n], xbuf.at[t, n], x_recv.at[t, n]).wait()
             weight_copy(t, n, down_qkv).wait()
             x = xbuf[t, n]
             xf = x.astype(F32)
-            square += jnp.sum(xf * xf, axis=-1, keepdims=True)
-            logits += mm_nt(x, wg[t, :, n * COLS : (n + 1) * COLS])
-            if n == CH - 1:
-                power = square * (1.0 / WIDTH) + EPSILON
-                rstd = lax.rsqrt(power)
-                beta, cum = gate_values(logits * rstd, rates_of(t))
+            x2 = (xf * xf).astype(BF)
+            square += mm(x2, ones)
+            square_row += mm_nt(ones[0 : 2 * HEADS, 0:DIM], x2[:, 0:DIM])
+            square_row += mm_nt(ones[0 : 2 * HEADS, 0:DIM], x2[:, DIM:COLS])
+            logits += mm_nt(wg[t, :, n * COLS : (n + 1) * COLS], x)
             for j in range(6):
                 block = slice(512 * j, 512 * (j + 1))
                 product = mm(x, wqkv[t, n * COLS : (n + 1) * COLS, block])
@@ -368,9 +377,10 @@
                 else:
                     proj[:, block] += product
 
-        @pl.when(t == 0)
-        def _():
-            load(1)
+        power = square * (1.0 / WIDTH) + EPSILON
+        scale = lax.rsqrt(square_row * (1.0 / WIDTH) + EPSILON)
+        gates = gate_rows(logits * scale, rates[t], triangle[...])
+
 
         masks = [maskb[level] for level in range(4)]
         low = maskb[4]
@@ -386,8 +396,12 @@
             bsend[t, h] = kx[:, DIM:TOK].astype(BF)
 
         floor[...] = head_maps(
-            range(HEADS), proj, rstd, power, beta, cum, select[...], masks, low, eye, put
-        )
+            proj, power, gates, select[...], masks, low, eye, put
+        )
+
+        @pl.when(t == 0)
+        def _():
+            load(1)
 
         @pl.when((t == 0) & outer)
         def _():
@@ -429,13 +443,18 @@
 
             s = sin[t, h]
             sout[t, h] = (mm(mmap[h], s) + bmap[h]).astype(BF)
-            obuf[h % 2] = mm(pmap[h], s) + rmap[h]
-            if h > 0:
+            if h < HEADS - 1:
+                obuf[h % 2] = mm(pmap[h], s) + rmap[h]
+                if h > 0:
+                    finish_head(h - 1)
+
+            @pl.when((c > 0) & (c < spans - 1))
+            def _():
+                state_copy(t, h).start()
+
+            if h == HEADS - 1:
+                obuf[h % 2] = mm(pmap[h], s) + rmap[h]
                 finish_head(h - 1)
-
-            @pl.when((c > 0) & (c < spans - 1))
-            def _():
-                state_copy(t, h).start()
 
             if h > 0:
                 send_pieces(h - 1)
@@ -592,7 +611,9 @@
         scratch_shapes=[
             pltpu.VMEM((2, WIDTH, 3 * WIDTH), BF),
             pltpu.VMEM((2, WIDTH, WIDTH), BF),
-            pltpu.VMEM((2, DIM, WIDTH), BF),
+            pltpu.VMEM((2, 2 * HEADS, WIDTH), BF),
+            pltpu.VMEM((2, 2 * HEADS, TOK), F32),
+            pltpu.VMEM((TOK, TOK), BF),
             pltpu.VMEM((2, CH, TOK, COLS), BF),
             pltpu.VMEM((2, CH, TOK, COLS), BF),
             pltpu.VMEM((TOK, 3 * WIDTH), F32),

time: 101 us -> 100 us (0.990)
  no operation moved by 1% of the time
where the time goes in v6:
time: 100 us
  Pallas kernels  99.7 us (100%)
    pallas_call x1, Pallas kernels, per_device(): pl.pallas_call(functools.partial(kernel, dims), out_shape=(jax.ShapeDtype...  97.6 us
    pallas_call x1, Pallas kernels, per_device(): pl.pallas_call(hand_over, out_shape=tuple((jax.ShapeDtypeStruct(a.shape,...  2.04 us

profile of v6, /device:TPU:37, one launch (start us, length us, event | category | flops | bytes accessed | tf_op | source)
XLA Modules:
  0.0 100.3 jit_solution(4935151464938489636)
XLA Ops:
  0.6 97.6 %shard_map.139 = (bf16[1,1,256,1024]{3,2,1,0:T(8,128)(2,1)}, bf16[1,1,256,1024]{3,2,1,0:T(8,128)(2,1)}, f32[1,32,1024]{2,1,0:T(8,128)}) custom-call(bf16[1,256,1024]{2,1,0:T(8,128)(2,1)} %down_in.1, bf16[1,256,1024]{2,1,0:T(8,128)(2,1)} %up_in.1, bf16[1,1024,3072]{2,1,0:T(8,128)(2,1)} %down_qkv.1, bf16[1,1024,3072]{2,1,0:T(8,128)(2,1)} %up_qkv.1, ...), custom_call_target="tpu_custom_call" | custom-call | tf_op jit(solution)/shard_map/pallas_call | solution.py:602
  98.3 2.0 %shard_map.140 = (bf16[1,1,256,1024]{3,2,1,0:T(8,128)(2,1)}, bf16[1,1,256,1024]{3,2,1,0:T(8,128)(2,1)}, f32[1,32,1024]{2,1,0:T(8,128)}) custom-call(bf16[1,1,256,1024]{3,2,1,0:T(8,128)(2,1)} %get-tuple-element.6.down_in, bf16[1,1,256,1024]{3,2,1,0:T(8,128)(2,1)} %get-tuple-element.7.up_in, f32[1,32,1024]{2,1,0:T(8,128)} %get-tuple-element.8.grad_in), custom_call_target="tpu_custom_call" | custom-call | tf_op jit(solution)/shard_map/pallas_call | solution.py:658

commit v7 on v6

--- a/solution.py
+++ b/solution.py
@@ -19,7 +19,7 @@
 CH = 4
 COLS = WIDTH // CH
 UNIT = 32
-PIECES = 4
+PIECES = ((0, 2), (2, 4), (4, 6), (6, 7), (7, 8))
 HANDS = 2
 
 
@@ -148,9 +148,9 @@
     down_in, up_in, down_qkv, up_qkv, down_gates, up_gates, down_rates, up_rates,
     down_wo, up_wo, down_ct, up_ct,
     down_out, up_out, grad_out,
-    wqkv, wo, wg, rates, triangle, xbuf, ybuf, proj, hid, obuf, maskb, select, floor, pmap, rmap, mmap, bmap, bsend, sin, sout,
+    wqkv, wo, wg, rate_in, rates, triangle, xbuf, ybuf, proj, hid, obuf, maskb, select, floor, pmap, rmap, mmap, bmap, bsend, sin, sout,
     cot, ht, hg, part, gbuf, gsum,
-    w_sem, wo_sem, x_recv, x_send, y_sem, s_recv, s_send, ct_recv, ct_send,
+    gate_sem, w_sem, wo_sem, x_recv, x_send, y_sem, s_recv, s_send, ct_recv, ct_send,
     ct_own, h_recv, h_send, g_recv, g_send, go_sem,
 ):
     sections, spans, copies = dims
@@ -206,6 +206,23 @@
         @pl.when(jnp.logical_not(is_down(t)))
         def _():
             start_weights(t, up_qkv, up_wo)
+
+    def gate_copies(t, gates, rate):
+        return (
+            pltpu.make_async_copy(gates.at[0], wg.at[t], gate_sem.at[t, 0]),
+            pltpu.make_async_copy(rate, rate_in.at[t], gate_sem.at[t, 1]),
+        )
+
+    for t in range(2):
+        @pl.when(is_down(t))
+        def _():
+            for copy in gate_copies(t, down_gates, down_rates):
+                copy.start()
+
+        @pl.when(jnp.logical_not(is_down(t)))
+        def _():
+            for copy in gate_copies(t, up_gates, up_rates):
+                copy.start()
 
     load(0)
 
@@ -226,17 +243,16 @@
     for h in range(HEADS):
         lanes = lax.broadcasted_iota(jnp.int32, (DIM, DIM), 1)
         select[h * DIM : (h + 1) * DIM] = (lanes == HEADS + h).astype(F32).astype(BF)
-    for t in range(2):
-        wg[t] = jnp.where(is_down(t), down_gates[0], up_gates[0])
-        rate = jnp.where(is_down(t), down_rates[...], up_rates[...])
-        rate = jnp.concatenate(
-            [jnp.zeros((1, HEADS), F32), rate, jnp.zeros((1, DIM - 2 * HEADS), F32)], axis=1
-        )
-        rate = jnp.broadcast_to(rate, (TOK, DIM)).T
-        rates[t] = rate[0 : 2 * HEADS]
     token = lax.broadcasted_iota(jnp.int32, (TOK, TOK), 0)
     until = lax.broadcasted_iota(jnp.int32, (TOK, TOK), 1)
     triangle[...] = (token <= until).astype(F32).astype(BF)
+    for t in range(2):
+        for copy in gate_copies(t, down_gates, down_rates):
+            copy.wait()
+        rate = jnp.concatenate(
+            [jnp.zeros((1, HEADS), F32), rate_in[t], jnp.zeros((1, DIM - 2 * HEADS), F32)], axis=1
+        )
+        rates[t] = jnp.broadcast_to(rate, (TOK, DIM)).T[0 : 2 * HEADS]
 
     half = TOK // 2
     before, after = lax.rem(d + copies - 1, copies), lax.rem(d + 1, copies)
@@ -327,15 +343,19 @@
             ybuf.at[t, n], out.at[0, 0, :, pl.ds(n * COLS, COLS)], y_sem.at[t, n]
         )
 
+    def piece_rows(piece):
+        first, end = (spans * share // HEADS * head for head in PIECES[piece])
+        return pl.ds(first, end - first)
+
     def hidden_own(t, piece):
-        rows = pl.ds(piece * (spans * share // PIECES), spans * share // PIECES)
+        rows = piece_rows(piece)
         return pltpu.make_async_copy(
             ht.at[t, d, rows], hg.at[t, d, rows], h_recv.at[t, d, piece]
         )
 
     def hidden_copy(t, k, piece):
         to = lax.rem(d + k, copies)
-        rows = pl.ds(piece * (spans * share // PIECES), spans * share // PIECES)
+        rows = piece_rows(piece)
         return remote(
             ht.at[t, to, rows], hg.at[t, d, rows], h_send.at[t, k - 1, piece],
             h_recv.at[t, d, piece], at(p, c, to),
@@ -429,9 +449,8 @@
                 ]
 
         def send_pieces(h):
-            for piece in range(PIECES):
-                last = HEADS // PIECES * (piece + 1) - 1 if spans == HEADS else HEADS - 1
-                if last == h:
+            for piece, (_, end) in enumerate(PIECES):
+                if h == (end - 1 if spans == HEADS else HEADS - 1):
                     hidden_own(t, piece).start()
                     for k in range(1, copies):
                         hidden_copy(t, k, piece).start()
@@ -471,12 +490,14 @@
             def _():
                 stream_copy(t, n).start()
 
-            @pl.when(is_down(t))
-            def _():
+        @pl.when(is_down(t))
+        def _():
+            for n in range(CH):
                 result_copy(t, n, down_out).start()
 
-            @pl.when(jnp.logical_not(is_down(t)))
-            def _():
+        @pl.when(jnp.logical_not(is_down(t)))
+        def _():
+            for n in range(CH):
                 result_copy(t, n, up_out).start()
 
         @pl.when(t == 0)
@@ -493,19 +514,19 @@
 
     def gradient(t):
         wait_cots(t)
-        size = spans * share // PIECES
-        for piece in range(PIECES):
-            rows = pl.ds(piece * size, size)
+        for piece in range(len(PIECES)):
+            rows = piece_rows(piece)
+            start, size = rows.start, rows.size
             for j in range(copies):
                 pltpu.make_async_copy(
                     hg.at[t, j, rows], hg.at[t, j, rows], h_recv.at[t, j, piece]
                 ).wait()
-            total = mm(hg[t, 0, piece * size : (piece + 1) * size], cot[t, 0])
+            total = mm(hg[t, 0, start : start + size], cot[t, 0])
             for j in range(1, copies):
-                total += mm(hg[t, j, piece * size : (piece + 1) * size], cot[t, j])
+                total += mm(hg[t, j, start : start + size], cot[t, j])
             total = total.astype(BF)
             for row0 in range(0, size, UNIT):
-                to, at_row = divmod(piece * size + row0, share)
+                to, at_row = divmod(start + row0, share)
                 part[t, to, at_row : at_row + UNIT] = total[row0 : row0 + UNIT]
                 if at_row + UNIT == share:
                     @pl.when(stays(t, to))
@@ -563,7 +584,7 @@
             if copies == 4:
                 cot_relay(t, way, to).wait_send()
         for k in range(1, copies):
-            for piece in range(PIECES):
+            for piece in range(len(PIECES)):
                 hidden_copy(t, k, piece).wait_send()
         for to in range(spans):
             @pl.when(jnp.logical_not(stays(t, to)))
@@ -597,7 +618,6 @@
     sections, spans, copies = dims
     share = WIDTH // (spans * copies)
     hbm = pl.BlockSpec(memory_space=pl.ANY)
-    vmem = pl.BlockSpec(memory_space=pltpu.VMEM)
     dma = pltpu.SemaphoreType.DMA
     down_acts, up_acts, grad = pl.pallas_call(
         functools.partial(kernel, dims),
@@ -606,12 +626,13 @@
             jax.ShapeDtypeStruct((1, 1, TOK, WIDTH), BF),
             jax.ShapeDtypeStruct((1, share, WIDTH), F32),
         ),
-        in_specs=[hbm] * 4 + [vmem] * 4 + [hbm] * 4,
+        in_specs=[hbm] * 12,
         out_specs=(hbm, hbm, hbm),
         scratch_shapes=[
             pltpu.VMEM((2, WIDTH, 3 * WIDTH), BF),
             pltpu.VMEM((2, WIDTH, WIDTH), BF),
             pltpu.VMEM((2, 2 * HEADS, WIDTH), BF),
+            pltpu.VMEM((2, 1, HEADS), F32),
             pltpu.VMEM((2, 2 * HEADS, TOK), F32),
             pltpu.VMEM((TOK, TOK), BF),
             pltpu.VMEM((2, CH, TOK, COLS), BF),
@@ -635,6 +656,7 @@
             pltpu.VMEM((2, spans, share, WIDTH), BF),
             pltpu.VMEM((2 * spans, share, WIDTH), BF),
             pltpu.VMEM((share, WIDTH), F32),
+            dma((2, 2)),
             dma((2, CH)),
             dma((2,)),
             dma((2, CH)),
@@ -645,8 +667,8 @@
             dma((2, 4)),
             dma((2, 4)),
             dma((2,)),
-            dma((2, copies, PIECES)),
-            dma((2, copies, PIECES)),
+            dma((2, copies, len(PIECES))),
+            dma((2, copies, len(PIECES))),
             dma((2 * spans,)),
             dma((2, spans)),
             dma,

time: 100 us -> 101 us (1.010)
  no operation moved by 1% of the time
where the time goes in v7:
time: 101 us
  Pallas kernels  100 us (99%)
    pallas_call x1, Pallas kernels, per_device(): pl.pallas_call(functools.partial(kernel, dims), out_shape=(jax.ShapeDtype...  98.2 us
    pallas_call x1, Pallas kernels, per_device(): pl.pallas_call(hand_over, out_shape=tuple((jax.ShapeDtypeStruct(a.shape,...  2.04 us

profile of v7, /device:TPU:37, one launch (start us, length us, event | category | flops | bytes accessed | tf_op | source)
XLA Modules:
  0.0 100.9 jit_solution(6637756295156889354)
XLA Ops:
  0.6 98.2 %shard_map.139 = (bf16[1,1,256,1024]{3,2,1,0:T(8,128)(2,1)}, bf16[1,1,256,1024]{3,2,1,0:T(8,128)(2,1)}, f32[1,32,1024]{2,1,0:T(8,128)}) custom-call(bf16[1,256,1024]{2,1,0:T(8,128)(2,1)} %down_in.1, bf16[1,256,1024]{2,1,0:T(8,128)(2,1)} %up_in.1, bf16[1,1024,3072]{2,1,0:T(8,128)(2,1)} %down_qkv.1, bf16[1,1024,3072]{2,1,0:T(8,128)(2,1)} %up_qkv.1, ...), custom_call_target="tpu_custom_call" | custom-call | tf_op jit(solution)/shard_map/pallas_call | solution.py:622
  98.8 2.0 %shard_map.140 = (bf16[1,1,256,1024]{3,2,1,0:T(8,128)(2,1)}, bf16[1,1,256,1024]{3,2,1,0:T(8,128)(2,1)}, f32[1,32,1024]{2,1,0:T(8,128)}) custom-call(bf16[1,1,256,1024]{3,2,1,0:T(8,128)(2,1)} %get-tuple-element.6.down_in, bf16[1,1,256,1024]{3,2,1,0:T(8,128)(2,1)} %get-tuple-element.7.up_in, f32[1,32,1024]{2,1,0:T(8,128)} %get-tuple-element.8.grad_in), custom_call_target="tpu_custom_call" | custom-call | tf_op jit(solution)/shard_map/pallas_call | solution.py:680

commit v8 on v7

--- a/solution.py
+++ b/solution.py
@@ -19,8 +19,7 @@
 CH = 4
 COLS = WIDTH // CH
 UNIT = 32
-PIECES = ((0, 2), (2, 4), (4, 6), (6, 7), (7, 8))
-HANDS = 2
+PIECES = ((0, 2), (2, 4), (4, 6), (6, 8))
 
 
 def mm(a, b):
@@ -147,11 +146,11 @@
     dims,
     down_in, up_in, down_qkv, up_qkv, down_gates, up_gates, down_rates, up_rates,
     down_wo, up_wo, down_ct, up_ct,
-    down_out, up_out, grad_out,
-    wqkv, wo, wg, rate_in, rates, triangle, xbuf, ybuf, proj, hid, obuf, maskb, select, floor, pmap, rmap, mmap, bmap, bsend, sin, sout,
-    cot, ht, hg, part, gbuf, gsum,
-    gate_sem, w_sem, wo_sem, x_recv, x_send, y_sem, s_recv, s_send, ct_recv, ct_send,
-    ct_own, h_recv, h_send, g_recv, g_send, go_sem,
+    ybuf, gsum,
+    wqkv, wo, wg, rate_in, rates, triangle, xbuf, proj, hid, obuf, maskb, select, floor, pmap, rmap, mmap, bmap, bsend, sin, sout,
+    cot, ht, hg, part, gbuf,
+    gate_sem, w_sem, wo_sem, x_recv, x_send, s_recv, s_send, ct_recv, ct_send,
+    ct_own, h_recv, h_send, g_recv, g_send,
 ):
     sections, spans, copies = dims
     p, c, d = lax.axis_index("pipe"), lax.axis_index("ctx"), lax.axis_index("dp")
@@ -335,13 +334,11 @@
         slot = jnp.where(stage_of(t) == 0, 0, 1)
         to = jnp.clip(jnp.where(is_down(t), p + 1, p - 1), 0, sections - 1)
         return remote(
-            ybuf.at[t, n], xbuf.at[slot, n], x_send.at[t, n], x_recv.at[slot, n], at(to, c, d)
-        )
-
-    def result_copy(t, n, out):
-        return pltpu.make_async_copy(
-            ybuf.at[t, n], out.at[0, 0, :, pl.ds(n * COLS, COLS)], y_sem.at[t, n]
-        )
+            ybuf.at[half_of(t), n], xbuf.at[slot, n], x_send.at[t, n], x_recv.at[slot, n], at(to, c, d)
+        )
+
+    def half_of(t):
+        return jnp.where(is_down(t), 0, 1)
 
     def piece_rows(piece):
         first, end = (spans * share // HEADS * head for head in PIECES[piece])
@@ -484,21 +481,11 @@
         for n in range(CH):
             block = slice(n * COLS, (n + 1) * COLS)
             y = xbuf[t, n].astype(F32) + mm(hid[...], wo[t, :, block])
-            ybuf[t, n] = y.astype(BF)
+            ybuf[half_of(t), n] = y.astype(BF)
 
             @pl.when(stage_of(t) < sections - 1)
             def _():
                 stream_copy(t, n).start()
-
-        @pl.when(is_down(t))
-        def _():
-            for n in range(CH):
-                result_copy(t, n, down_out).start()
-
-        @pl.when(jnp.logical_not(is_down(t)))
-        def _():
-            for n in range(CH):
-                result_copy(t, n, up_out).start()
 
         @pl.when(t == 0)
         def _():
@@ -562,14 +549,10 @@
     total = gbuf[0].astype(F32)
     for j in range(1, 2 * spans):
         total += gbuf[j].astype(F32)
-    gsum[...] = total
-    final = pltpu.make_async_copy(gsum, grad_out.at[0], go_sem)
-    final.start()
+    gsum[0] = total
 
     for t in range(2):
         for n in range(CH):
-            result_copy(t, n, down_out).wait()
-
             @pl.when(stage_of(t) < sections - 1)
             def _():
                 stream_copy(t, n).wait_send()
@@ -591,43 +574,33 @@
             def _():
                 grad_copy(t, to).wait_send()
 
-    final.wait()
-
-
-def hand_over(down_in, up_in, grad_in, down_out, up_out, grad_out, acts, grad, in_sems, out_sems):
-    rows = TOK // HANDS
-    moves = []
-    for i, (src, dst) in enumerate(((down_in, down_out), (up_in, up_out))):
-        for n in range(HANDS):
-            part = (0, 0, pl.ds(n * rows, rows))
-            moves.append((src.at[part], acts.at[i, pl.ds(n * rows, rows)], dst.at[part]))
-    moves.append((grad_in.at[0], grad, grad_out.at[0]))
-    loads, stores = [], []
-    for i, (src, here, dst) in enumerate(moves):
-        loads.append(pltpu.make_async_copy(src, here, in_sems.at[i]))
-        stores.append(pltpu.make_async_copy(here, dst, out_sems.at[i]))
-        loads[i].start()
-    for load, store in zip(loads, stores):
-        load.wait()
-        store.start()
-    for store in stores:
-        store.wait()
+
+def hand_over(acts, grad, down_out, up_out, grad_out, sems):
+    moves = [pltpu.make_async_copy(grad, grad_out, sems.at[2 * CH])]
+    for i, out in enumerate((down_out, up_out)):
+        for n in range(CH):
+            to = out.at[0, 0, :, pl.ds(n * COLS, COLS)]
+            moves.append(pltpu.make_async_copy(acts.at[i, n], to, sems.at[i * CH + n]))
+    for move in moves:
+        move.start()
+    for move in moves:
+        move.wait()
 
 
 def per_device(dims, *arrays):
     sections, spans, copies = dims
     share = WIDTH // (spans * copies)
     hbm = pl.BlockSpec(memory_space=pl.ANY)
+    vmem = pl.BlockSpec(memory_space=pltpu.VMEM)
     dma = pltpu.SemaphoreType.DMA
-    down_acts, up_acts, grad = pl.pallas_call(
+    acts, grad = pl.pallas_call(
         functools.partial(kernel, dims),
         out_shape=(
-            jax.ShapeDtypeStruct((1, 1, TOK, WIDTH), BF),
-            jax.ShapeDtypeStruct((1, 1, TOK, WIDTH), BF),
-            jax.ShapeDtypeStruct((1, share, WIDTH), F32),
+            pltpu.VMEM((2, CH, TOK, COLS), BF),
+            pltpu.VMEM((1, share, WIDTH), F32),
         ),
         in_specs=[hbm] * 12,
-        out_specs=(hbm, hbm, hbm),
+        out_specs=(vmem, vmem),
         scratch_shapes=[
             pltpu.VMEM((2, WIDTH, 3 * WIDTH), BF),
             pltpu.VMEM((2, WIDTH, WIDTH), BF),
@@ -635,7 +608,6 @@
             pltpu.VMEM((2, 1, HEADS), F32),
             pltpu.VMEM((2, 2 * HEADS, TOK), F32),
             pltpu.VMEM((TOK, TOK), BF),
-            pltpu.VMEM((2, CH, TOK, COLS), BF),
             pltpu.VMEM((2, CH, TOK, COLS), BF),
             pltpu.VMEM((TOK, 3 * WIDTH), F32),
             pltpu.VMEM((TOK, WIDTH), BF),
@@ -655,11 +627,9 @@
             pltpu.VMEM((2, copies, spans * share, TOK), BF),
             pltpu.VMEM((2, spans, share, WIDTH), BF),
             pltpu.VMEM((2 * spans, share, WIDTH), BF),
-            pltpu.VMEM((share, WIDTH), F32),
             dma((2, 2)),
             dma((2, CH)),
             dma((2,)),
-            dma((2, CH)),
             dma((2, CH)),
             dma((2, CH)),
             dma((2, HEADS)),
@@ -671,7 +641,6 @@
             dma((2, copies, len(PIECES))),
             dma((2 * spans,)),
             dma((2, spans)),
-            dma,
         ],
         compiler_params=pltpu.CompilerParams(
             collective_id=0, has_side_effects=True, vmem_limit_bytes=60 * 1024 * 1024
@@ -679,16 +648,15 @@
     )(*arrays[:4], *(jnp.swapaxes(gates, 1, 2) for gates in arrays[4:6]), *arrays[6:])
     return pl.pallas_call(
         hand_over,
-        out_shape=tuple(jax.ShapeDtypeStruct(a.shape, a.dtype) for a in (down_acts, up_acts, grad)),
-        in_specs=[hbm] * 3,
+        out_shape=(
+            jax.ShapeDtypeStruct((1, 1, TOK, WIDTH), BF),
+            jax.ShapeDtypeStruct((1, 1, TOK, WIDTH), BF),
+            jax.ShapeDtypeStruct((1, share, WIDTH), F32),
+        ),
+        in_specs=[vmem] * 2,
         out_specs=(hbm, hbm, hbm),
-        scratch_shapes=[
-            pltpu.VMEM((2, TOK, WIDTH), BF),
-            pltpu.VMEM((share, WIDTH), F32),
-            dma((2 * HANDS + 1,)),
-            dma((2 * HANDS + 1,)),
-        ],
-    )(down_acts, up_acts, grad)
+        scratch_shapes=[dma((2 * CH + 1,))],
+    )(acts, grad)
 
 
 def solution(mesh):

time: 101 us -> 102 us (level)
  local copies, waits for them, and re-layouts: 0 us -> 1.61 us
    unnamed x0 -> x4, local copies, waits for them, and re-layouts: none -> 1.61 us
where the time goes in v8:
time: 102 us
  Pallas kernels  100 us (98%)
  local copies, waits for them, and re-layouts  1.61 us (2%)
    pallas_call x1, Pallas kernels, per_device(): pl.pallas_call(functools.partial(kernel, dims), out_shape=(pltpu.VMEM((2,...  97.7 us
    pallas_call x1, Pallas kernels, per_device(): pl.pallas_call(hand_over, out_shape=(jax.ShapeDtypeStruct((1, 1, TOK, WID...  2.3 us

profile of v8, /device:TPU:37, one launch (start us, length us, event | category | flops | bytes accessed | tf_op | source)
XLA Modules:
  0.0 102.3 jit_solution(12638683045001250445)
XLA Ops:
  0.6 97.7 %shard_map.139 = (bf16[2,4,256,256]{3,2,1,0:T(8,128)(2,1)S(1)}, f32[1,32,1024]{2,1,0:T(8,128)S(1)}) custom-call(bf16[1,256,1024]{2,1,0:T(8,128)(2,1)} %down_in.1, bf16[1,256,1024]{2,1,0:T(8,128)(2,1)} %up_in.1, bf16[1,1024,3072]{2,1,0:T(8,128)(2,1)} %down_qkv.1, bf16[1,1024,3072]{2,1,0:T(8,128)(2,1)} %up_qkv.1, bf16[1,16,1024]{2,1,0:T(8,128)(2,1)} %bitcast.2, ...), custom_call_target="tpu_custom_call" | custom-call | tf_op jit(solution)/shard_map/pallas_call | solution.py:596
  98.3 0.0 copy-start
  98.3 1.0 copy-done
  99.3 0.0 copy-start.1
  99.3 0.6 copy-done.1
  100.0 2.3 %shard_map.140 = (bf16[1,1,256,1024]{3,2,1,0:T(8,128)(2,1)}, bf16[1,1,256,1024]{3,2,1,0:T(8,128)(2,1)}, f32[1,32,1024]{2,1,0:T(8,128)}) custom-call(bf16[2,4,256,256]{3,2,1,0:T(8,128)(2,1)} %copy-done, f32[1,32,1024]{2,1,0:T(8,128)} %copy-done.1), custom_call_target="tpu_custom_call" | custom-call | tf_op jit(solution)/shard_map/pallas_call | solution.py:649
Async XLA Ops:
  98.3 1.0 copy-start
  99.3 0.6 copy-start.1

commit v9 on v6

--- a/solution.py
+++ b/solution.py
@@ -181,7 +181,8 @@
     def start_weights(t, qkv, out):
         for n in range(CH):
             weight_copy(t, n, qkv).start()
-        out_copy(t, out).start()
+        if t == 1:
+            out_copy(t, out).start()
 
     def input_copy(src, n):
         return pltpu.make_async_copy(
@@ -401,6 +402,14 @@
 
         @pl.when(t == 0)
         def _():
+            @pl.when(low_half)
+            def _():
+                out_copy(0, down_wo).start()
+
+            @pl.when(jnp.logical_not(low_half))
+            def _():
+                out_copy(0, up_wo).start()
+
             load(1)
 
         @pl.when((t == 0) & outer)
@@ -433,7 +442,7 @@
                 last = HEADS // PIECES * (piece + 1) - 1 if spans == HEADS else HEADS - 1
                 if last == h:
                     hidden_own(t, piece).start()
-                    for k in range(1, copies):
+                    for k in sorted(range(1, copies), key=lambda k: abs(2 * k - copies)):
                         hidden_copy(t, k, piece).start()
 
         for h in range(HEADS):
@@ -471,12 +480,14 @@
             def _():
                 stream_copy(t, n).start()
 
-            @pl.when(is_down(t))
-            def _():
+        @pl.when(is_down(t))
+        def _():
+            for n in range(CH):
                 result_copy(t, n, down_out).start()
 
-            @pl.when(jnp.logical_not(is_down(t)))
-            def _():
+        @pl.when(jnp.logical_not(is_down(t)))
+        def _():
+            for n in range(CH):
                 result_copy(t, n, up_out).start()
 
         @pl.when(t == 0)

time: 100 us -> 101 us (1.010)
  no operation moved by 1% of the time
where the time goes in v9:
time: 101 us; the launch traced here: 100 us
  Pallas kernels  99.8 us (99%)
    pallas_call x1, Pallas kernels, per_device(): pl.pallas_call(functools.partial(kernel, dims), out_shape=(jax.ShapeDtype...  97.8 us
    pallas_call x1, Pallas kernels, per_device(): pl.pallas_call(hand_over, out_shape=tuple((jax.ShapeDtypeStruct(a.shape,...  2.04 us

profile of v9, /device:TPU:37, one launch (start us, length us, event | category | flops | bytes accessed | tf_op | source)
XLA Modules:
  0.0 100.5 jit_solution(714299898835028963)
XLA Ops:
  0.6 97.8 %shard_map.139 = (bf16[1,1,256,1024]{3,2,1,0:T(8,128)(2,1)}, bf16[1,1,256,1024]{3,2,1,0:T(8,128)(2,1)}, f32[1,32,1024]{2,1,0:T(8,128)}) custom-call(bf16[1,256,1024]{2,1,0:T(8,128)(2,1)} %down_in.1, bf16[1,256,1024]{2,1,0:T(8,128)(2,1)} %up_in.1, bf16[1,1024,3072]{2,1,0:T(8,128)(2,1)} %down_qkv.1, bf16[1,1024,3072]{2,1,0:T(8,128)(2,1)} %up_qkv.1, ...), custom_call_target="tpu_custom_call" | custom-call | tf_op jit(solution)/shard_map/pallas_call | solution.py:613
  98.4 2.0 %shard_map.140 = (bf16[1,1,256,1024]{3,2,1,0:T(8,128)(2,1)}, bf16[1,1,256,1024]{3,2,1,0:T(8,128)(2,1)}, f32[1,32,1024]{2,1,0:T(8,128)}) custom-call(bf16[1,1,256,1024]{3,2,1,0:T(8,128)(2,1)} %get-tuple-element.6.down_in, bf16[1,1,256,1024]{3,2,1,0:T(8,128)(2,1)} %get-tuple-element.7.up_in, f32[1,32,1024]{2,1,0:T(8,128)} %get-tuple-element.8.grad_in), custom_call_target="tpu_custom_call" | custom-call | tf_op jit(solution)/shard_map/pallas_call | solution.py:669

commit v10 on v9

--- a/solution.py
+++ b/solution.py
@@ -363,6 +363,15 @@
         for n in range(CH):
             pltpu.make_async_copy(xbuf.at[t, n], xbuf.at[t, n], x_recv.at[t, n]).wait()
             weight_copy(t, n, down_qkv).wait()
+            if n == CH - 1:
+                @pl.when((t == 0) & low_half)
+                def _():
+                    out_copy(0, down_wo).start()
+
+                @pl.when((t == 0) & jnp.logical_not(low_half))
+                def _():
+                    out_copy(0, up_wo).start()
+
             x = xbuf[t, n]
             xf = x.astype(F32)
             x2 = (xf * xf).astype(BF)
@@ -402,14 +411,6 @@
 
         @pl.when(t == 0)
         def _():
-            @pl.when(low_half)
-            def _():
-                out_copy(0, down_wo).start()
-
-            @pl.when(jnp.logical_not(low_half))
-            def _():
-                out_copy(0, up_wo).start()
-
             load(1)
 
         @pl.when((t == 0) & outer)

time: 101 us -> 100 us (0.990)
  no operation moved by 1% of the time
where the time goes in v10:
time: 100 us
  Pallas kernels  99.5 us (100%)
    pallas_call x1, Pallas kernels, per_device(): pl.pallas_call(functools.partial(kernel, dims), out_shape=(jax.ShapeDtype...  97.5 us
    pallas_call x1, Pallas kernels, per_device(): pl.pallas_call(hand_over, out_shape=tuple((jax.ShapeDtypeStruct(a.shape,...  2.04 us

profile of v10, /device:TPU:37, one launch (start us, length us, event | category | flops | bytes accessed | tf_op | source)
XLA Modules:
  0.0 100.1 jit_solution(13548671694856532854)
XLA Ops:
  0.6 97.5 %shard_map.139 = (bf16[1,1,256,1024]{3,2,1,0:T(8,128)(2,1)}, bf16[1,1,256,1024]{3,2,1,0:T(8,128)(2,1)}, f32[1,32,1024]{2,1,0:T(8,128)}) custom-call(bf16[1,256,1024]{2,1,0:T(8,128)(2,1)} %down_in.1, bf16[1,256,1024]{2,1,0:T(8,128)(2,1)} %up_in.1, bf16[1,1024,3072]{2,1,0:T(8,128)(2,1)} %down_qkv.1, bf16[1,1024,3072]{2,1,0:T(8,128)(2,1)} %up_qkv.1, ...), custom_call_target="tpu_custom_call" | custom-call | tf_op jit(solution)/shard_map/pallas_call | solution.py:614
  98.1 2.0 %shard_map.140 = (bf16[1,1,256,1024]{3,2,1,0:T(8,128)(2,1)}, bf16[1,1,256,1024]{3,2,1,0:T(8,128)(2,1)}, f32[1,32,1024]{2,1,0:T(8,128)}) custom-call(bf16[1,1,256,1024]{3,2,1,0:T(8,128)(2,1)} %get-tuple-element.6.down_in, bf16[1,1,256,1024]{3,2,1,0:T(8,128)(2,1)} %get-tuple-element.7.up_in, f32[1,32,1024]{2,1,0:T(8,128)} %get-tuple-element.8.grad_in), custom_call_target="tpu_custom_call" | custom-call | tf_op jit(solution)/shard_map/pallas_call | solution.py:670

commit v11 on v10

--- a/solution.py
+++ b/solution.py
@@ -20,7 +20,7 @@
 COLS = WIDTH // CH
 UNIT = 32
 PIECES = 4
-HANDS = 2
+HANDS = 4
 
 
 def mm(a, b):

time: 100 us -> 100 us (level)
  no operation moved by 1% of the time
where the time goes in v11:
time: 100 us
  Pallas kernels  99.6 us (100%)
    pallas_call x1, Pallas kernels, per_device(): pl.pallas_call(functools.partial(kernel, dims), out_shape=(jax.ShapeDtype...  97.5 us
    pallas_call x1, Pallas kernels, per_device(): pl.pallas_call(hand_over, out_shape=tuple((jax.ShapeDtypeStruct(a.shape,...  2.15 us

profile of v11, /device:TPU:37, one launch (start us, length us, event | category | flops | bytes accessed | tf_op | source)
XLA Modules:
  0.0 100.3 jit_solution(5983814154149600039)
XLA Ops:
  0.6 97.5 %shard_map.139 = (bf16[1,1,256,1024]{3,2,1,0:T(8,128)(2,1)}, bf16[1,1,256,1024]{3,2,1,0:T(8,128)(2,1)}, f32[1,32,1024]{2,1,0:T(8,128)}) custom-call(bf16[1,256,1024]{2,1,0:T(8,128)(2,1)} %down_in.1, bf16[1,256,1024]{2,1,0:T(8,128)(2,1)} %up_in.1, bf16[1,1024,3072]{2,1,0:T(8,128)(2,1)} %down_qkv.1, bf16[1,1024,3072]{2,1,0:T(8,128)(2,1)} %up_qkv.1, ...), custom_call_target="tpu_custom_call" | custom-call | tf_op jit(solution)/shard_map/pallas_call | solution.py:614
  98.1 2.1 %shard_map.140 = (bf16[1,1,256,1024]{3,2,1,0:T(8,128)(2,1)}, bf16[1,1,256,1024]{3,2,1,0:T(8,128)(2,1)}, f32[1,32,1024]{2,1,0:T(8,128)}) custom-call(bf16[1,1,256,1024]{3,2,1,0:T(8,128)(2,1)} %get-tuple-element.6.down_in, bf16[1,1,256,1024]{3,2,1,0:T(8,128)(2,1)} %get-tuple-element.7.up_in, f32[1,32,1024]{2,1,0:T(8,128)} %get-tuple-element.8.grad_in), custom_call_target="tpu_custom_call" | custom-call | tf_op jit(solution)/shard_map/pallas_call | solution.py:670
